TPU v7x, 256 devices: a whole 4x4x8 slice. The times are simulated.
256 devices in a mesh: dp: 32 (over y, x, z_lo), tensor: 8 (over z_hi, core).
Axes of the slice: x: 4, y: 4, z: 8 (z_hi: 4, z_lo: 2; z = z_hi * 2 + z_lo), core: 2. Of those that a mesh axis runs over, the one named last changes fastest.
Arguments:
- queries: bfloat16 [22528, 4096], P('dp', 'tensor'), may hold values from -6 to 6
- nb_states: bfloat16 [512, 128, 768], P('dp', 'tensor'), may hold values from -400 to 400
- nb_owner: int32 [352, 2], P('dp'), may hold values from 0 to 31, all different within a row; in each aligned block of 11 rows (0 to 10, 11 to 21, ...) at most 2 rows name the same one
- nb_row: int32 [352, 2], P('dp'), may hold values from 0 to 15
- enc_gain: float32 [768], replicated, may hold values from 0.1 to 1.9
- key_weight: bfloat16 [768, 4096], P(None, 'tensor'), may hold values from -0.21875 to 0.21875
- value_weight: bfloat16 [768, 4096], P(None, 'tensor'), may hold values from -0.21875 to 0.21875
- grad_attn: bfloat16 [22528, 4096], P('dp', 'tensor'), may hold values from -3 to 3
Outputs:
- attn_out: bfloat16 [22528, 4096], P('dp', 'tensor')
- grad_queries: bfloat16 [22528, 4096], P('dp', 'tensor')
- grad_states: bfloat16 [512, 128, 768], P('dp', 'tensor')
- grad_key_weight: float32 [768, 4096], P(None, 'tensor')
- grad_value_weight: float32 [768, 4096], P(None, 'tensor')
Inputs may be any that keep to these rules, and one draw needn't show every extreme that they name: `nb_owner`: the 2 neighbours of a span have different owners; among the 11 spans of one dp index no owner is named more than 2 times, a bound that some block reaches.
All inputs are finite; a program needn't handle non-finite values.
Results may differ from a plain program's by a relative error of at most 0.03.
Values may be sent and summed in bfloat16 or wider, within the bound.
A program may use at most 128 MiB of HBM per device.

v0:
```python
import jax
import jax.numpy as jnp
from jax import lax
from jax.sharding import PartitionSpec as P

HEAD_DIM = 128


epsilon = 1e-06


def normalize(values):
    widened = values.astype(jnp.float32)
    inverse = lax.rsqrt(jnp.mean(widened * widened, axis=-1, keepdims=True) + epsilon)
    return (widened * inverse, inverse)


def body(queries, nb_states, nb_owner, nb_row, enc_gain, key_weight, value_weight, grad_attn):
    groups = lax.axis_size("dp")
    owner_list = nb_owner.reshape(-1)
    row_list = nb_row.reshape(-1)
    asked_count = owner_list.shape[0]
    capacity = max(2, (2 * asked_count + groups - 1) // groups)
    positions = jnp.arange(asked_count, dtype=jnp.int32)
    same_owner = owner_list[:, None] == owner_list[None, :]
    before_me = positions[None, :] < positions[:, None]
    slot_rank = jnp.sum(jnp.where(same_owner & before_me, 1, 0), axis=1).astype(jnp.int32)
    slot_index = owner_list * capacity + slot_rank
    slot_count = groups * capacity
    selector = slot_index[:, None] == jnp.arange(slot_count, dtype=jnp.int32)[None, :]
    request = jnp.sum(jnp.where(selector, row_list[:, None], 0), axis=0).reshape(groups, capacity)
    asked_rows = lax.all_to_all(request, "dp", split_axis=0, concat_axis=0, tiled=True)
    asked_flat = asked_rows.reshape(-1)
    local_len = nb_states.shape[1]
    enc_width = nb_states.shape[2]
    outgoing = nb_states[asked_flat].reshape(groups, capacity, local_len, enc_width)
    fetched = lax.all_to_all(outgoing, "dp", split_axis=0, concat_axis=0, tiled=True)
    select_half = selector.astype(jnp.bfloat16)
    mine_states = jnp.dot(
        select_half,
        fetched.reshape(slot_count, local_len * enc_width),
        preferred_element_type=jnp.float32,
    )
    mine_states = mine_states.astype(jnp.bfloat16).reshape(asked_count, local_len, enc_width)
    unit_slice, inverse_slice = normalize(mine_states)
    gathered = lax.all_gather(mine_states, "tensor", axis=1, tiled=True)
    unit_all, inverse_all = normalize(gathered)
    encoded = (unit_all * enc_gain).astype(jnp.bfloat16)
    full_len = encoded.shape[1]
    flat_encoded = encoded.reshape(asked_count * full_len, enc_width)
    key_all = jnp.dot(flat_encoded, key_weight, preferred_element_type=jnp.float32).astype(
        jnp.bfloat16
    )
    value_all = jnp.dot(flat_encoded, value_weight, preferred_element_type=jnp.float32).astype(
        jnp.bfloat16
    )
    span_count = nb_owner.shape[0]
    per_span = nb_owner.shape[1]
    heads_here = key_weight.shape[1] // HEAD_DIM
    span_len = queries.shape[0] // span_count
    key_blocks = key_all.reshape(span_count, per_span * full_len, heads_here, HEAD_DIM)
    value_blocks = value_all.reshape(span_count, per_span * full_len, heads_here, HEAD_DIM)
    query_blocks = queries.reshape(span_count, span_len, heads_here, HEAD_DIM)
    grad_blocks = grad_attn.reshape(span_count, span_len, heads_here, HEAD_DIM)
    score_scale = HEAD_DIM ** (-0.5)
    scores = (
        jnp.einsum("cqhd,ckhd->chqk", query_blocks, key_blocks, preferred_element_type=jnp.float32)
        * score_scale
    )
    exponent = jnp.exp(scores)
    probabilities = exponent / jnp.sum(exponent, axis=-1, keepdims=True)
    weights = probabilities.astype(jnp.bfloat16)
    attn_out = jnp.einsum(
        "chqk,ckhd->cqhd", weights, value_blocks, preferred_element_type=jnp.float32
    )
    attn_out = attn_out.astype(jnp.bfloat16).reshape(queries.shape)
    grad_weights = jnp.einsum(
        "cqhd,ckhd->chqk", grad_blocks, value_blocks, preferred_element_type=jnp.float32
    )
    grad_scores = (
        probabilities
        * (grad_weights - jnp.sum(probabilities * grad_weights, axis=-1, keepdims=True))
        * score_scale
    ).astype(jnp.bfloat16)
    grad_queries = jnp.einsum(
        "chqk,ckhd->cqhd", grad_scores, key_blocks, preferred_element_type=jnp.float32
    )
    grad_queries = grad_queries.astype(jnp.bfloat16).reshape(queries.shape)
    grad_keys = jnp.einsum(
        "chqk,cqhd->ckhd", grad_scores, query_blocks, preferred_element_type=jnp.float32
    )
    grad_keys = grad_keys.astype(jnp.bfloat16).reshape(-1, key_weight.shape[1])
    grad_values = jnp.einsum(
        "chqk,cqhd->ckhd", weights, grad_blocks, preferred_element_type=jnp.float32
    )
    grad_values = grad_values.astype(jnp.bfloat16).reshape(-1, value_weight.shape[1])
    key_term = jnp.dot(flat_encoded.T, grad_keys, preferred_element_type=jnp.float32)
    value_term = jnp.dot(flat_encoded.T, grad_values, preferred_element_type=jnp.float32)
    grad_key_weight, grad_value_weight = (
        lax.psum(key_term.astype(jnp.bfloat16), "dp").astype(jnp.float32),
        lax.psum(value_term.astype(jnp.bfloat16), "dp").astype(jnp.float32),
    )
    enc_term = jnp.dot(grad_keys, key_weight.T, preferred_element_type=jnp.float32)
    enc_term = enc_term + jnp.dot(grad_values, value_weight.T, preferred_element_type=jnp.float32)
    enc_term = enc_term.reshape(asked_count, full_len, enc_width)
    summed_grad = lax.psum(enc_term.astype(jnp.bfloat16), "tensor").astype(jnp.float32)
    own_grad = lax.dynamic_slice_in_dim(
        summed_grad, lax.axis_index("tensor") * local_len, local_len, 1
    )
    scaled = own_grad * enc_gain
    grad_raw = (
        inverse_slice
        * (scaled - unit_slice * jnp.mean(scaled * unit_slice, axis=-1, keepdims=True))
    ).astype(jnp.bfloat16)
    outgoing_grad = jnp.dot(
        select_half.T,
        grad_raw.reshape(asked_count, local_len * enc_width),
        preferred_element_type=jnp.float32,
    )
    outgoing_grad = outgoing_grad.astype(jnp.bfloat16).reshape(
        groups, capacity, local_len, enc_width
    )
    returned = lax.all_to_all(outgoing_grad, "dp", split_axis=0, concat_axis=0, tiled=True)
    owned_count = nb_states.shape[0]
    owner_rows = (asked_flat[None, :] == jnp.arange(owned_count, dtype=jnp.int32)[:, None]).astype(
        jnp.bfloat16
    )
    grad_states = jnp.dot(
        owner_rows,
        returned.reshape(slot_count, local_len * enc_width),
        preferred_element_type=jnp.float32,
    )
    grad_states = grad_states.astype(jnp.bfloat16).reshape(nb_states.shape)
    return (attn_out, grad_queries, grad_states, grad_key_weight, grad_value_weight)


def solution(mesh):
    return jax.shard_map(
        body,
        mesh=mesh,
        in_specs=(
            P("dp", "tensor"),
            P("dp", "tensor", None),
            P("dp", None),
            P("dp", None),
            P(),
            P(None, "tensor"),
            P(None, "tensor"),
            P("dp", "tensor"),
        ),
        out_specs=(
            P("dp", "tensor"),
            P("dp", "tensor"),
            P("dp", "tensor", None),
            P(None, "tensor"),
            P(None, "tensor"),
        ),
        check_vma=False,
    )
```

profile of v0, /device:TPU:32, one launch (start us, length us, event | category | flops | bytes accessed | tf_op | source)
XLA Modules:
  0.0 658.2 jit_solution(16230823903540449889)
XLA Ops:
  7.2 0.0 all-gather.2.cloned.1.call-start
  7.2 0.8 copy.52
  8.1 0.1 reshape.135
  8.1 0.2 select_reduce_fusion.1
  8.3 0.8 copy.53
  9.1 0.1 broadcast_in_dim.24
  9.2 0.1 select_reduce_fusion
  9.3 0.1 all_to_all.12
  9.4 15.4 %all_to_all.19 = s32[32,1,2]{2,1,0:T(1,128)S(1)} all-to-all(s32[32,1,2]{2,1,0:T(1,128)S(1)} %bitcast.142), channel_id=1, replica_groups=mesh['dp'=32,'tensor'=8] {'dp'}, dimensions={0} | all-to-all | bytes 512 | tf_op jit(solution)/shard_map/all_to_all | solution.py:32
  24.8 0.5 broadcast.107
  25.3 0.7 reduce.5
  26.0 0.1 reshape.136
  26.2 1.6 gather_fusion
  27.8 25.4 %all_to_all.20 = bf16[32,2,16,768]{3,2,1,0:T(8,128)(2,1)S(1)} all-to-all(bf16[32,2,16,768]{3,2,1,0:T(8,128)(2,1)S(1)} %bitcast.124), channel_id=1, replica_groups=mesh['dp'=32,'tensor'=8] {'dp'}, dimensions={0} | all-to-all | bytes 3145728 | tf_op jit(solution)/shard_map/all_to_all | solution.py:37
  53.2 0.5 copy.67
  53.7 0.4 convolution_convert_fusion.1
  54.1 0.1 copy.68
  54.2 0.8 slice.2
  55.1 0.0 all-gather.2.cloned.1.call-update
  55.1 0.0 all-reduce.4.cloned.1.call-start
  55.1 0.2 reshape.143
  55.3 0.2 reshape.145
  55.5 52.6 %all-gather.2.cloned.1.call-done = bf16[22,128,768]{2,1,0:T(8,128)(2,1)} async-done(((bf16[22,16,768]{2,1,0:T(8,128)(2,1)}), bf16[22,128,768]{2,1,0:T(8,128)(2,1)}) %all-gather.2.cloned.1.call-update) | async-done | bytes 4325392 | tf_op jit(solution)/shard_map/all_gather | solution.py:46
  108.1 3.3 fusion.1
  111.4 0.2 copy-done.2
  111.6 1.7 fusion.3
  113.3 2.0 copy-done.3
  115.3 4.0 convolution_convert_fusion.3
  119.3 6.0 reshape.142
  125.3 6.4 convolution_convert_fusion.4
  131.7 5.9 reshape.141
  137.6 4.6 fusion.18
  142.3 1.2 bitcast_reduce_fusion
  143.5 1.6 copy-done.16
  145.1 3.0 convert_bitcast_fusion
  148.1 20.8 %convert_bitcast_fusion.1 = bf16[11,256,4,128]{3,1,2,0:T(8,128)(2,1)} fusion(f32[11,4,256,64]{2,3,1,0:T(8,128)} %fusion.18, bf16[11,64,4,128]{3,2,1,0:T(4,128)(2,1)S(1)} %reshape.143, f32[11,4,256,64]{2,3,1,0:T(8,128)} %copy-done.16, f32[11,4,64]{2,1,0:T(4,128)S(1)} %get-tuple-element.7), kind=kOutput, calls=%fused_computation.28 | convolution fusion | flops 192482304 | bytes 9382912 | tf_op jit(solution)/shard_map/chqk,cqhd->ckhd/dot_general | solution.py:89
  169.0 4.2 copy.66
  173.2 2.2 copy.64
  175.5 2.4 fusion.9
  177.9 4.5 add_convert_fusion
  182.4 0.0 all-reduce.4.cloned.1.call-update
  182.5 0.2 fusion.51
  182.7 115.6 %all-reduce.4.cloned.1.call-done = bf16[22,128,768]{2,1,0:T(8,128)(2,1)} async-done(((bf16[22,128,768]{2,1,0:T(8,128)(2,1)}), bf16[22,128,768]{2,1,0:T(8,128)(2,1)}) %all-reduce.4.cloned.1.call-update) | async-done | bytes 4325392 | tf_op jit(solution)/shard_map/psum | solution.py:106
  298.2 1.4 fusion.47
  299.6 1.4 fusion.50
  301.0 0.2 copy.73
  301.2 0.7 convolution_convert_fusion
  301.9 1.5 copy.74
  303.4 11.8 %all-to-all-start.2 = ((bf16[32,2,16,768]{3,2,1,0:T(8,128)(2,1)}), bf16[32,2,16,768]{3,2,1,0:T(8,128)(2,1)S(1)}, u32[]{:S(2)}, u32[]{:S(2)}) async-start(bf16[32,2,16,768]{3,2,1,0:T(8,128)(2,1)} %bitcast.119), calls=%async_computation.2 | async-start | bytes 3145728 | tf_op jit(solution)/shard_map/all_to_all | solution.py:123
  315.2 0.3 all-reduce.6.cloned.1.call-start
  315.5 6.6 fusion.26
  322.1 5.5 fusion.29
  327.6 0.1 eq.47
  327.7 3.6 fusion.40
  331.4 0.6 copy.58
  332.0 20.7 %fusion.43 = bf16[11,64,4,128]{3,1,2,0:T(8,128)(2,1)S(1)} fusion(bf16[11,256,4,128]{3,2,1,0:T(4,128)(2,1)} %reshape.142, f32[11,4,256,64]{2,3,1,0:T(8,128)} %fusion.18, f32[11,4,256,64]{2,3,1,0:T(8,128)} %copy-done.16, f32[11,4,64]{2,1,0:T(4,128)S(1)} %copy-done.18), kind=kOutput, calls=%fused_computation.51 | convolution fusion | flops 191400960 | bytes 9382912 | tf_op jit(solution)/shard_map/chqk,ckhd->cqhd/dot_general | solution.py:85
  352.7 0.6 copy.62
  353.3 1.4 copy_bitcast_fusion
  354.6 291.2 %all-reduce.6.cloned.1.call-done = (bf16[768,512]{1,0:T(8,128)(2,1)}, bf16[768,512]{1,0:T(8,128)(2,1)}) async-done(((bf16[768,512]{1,0:T(8,128)(2,1)}, bf16[768,512]{1,0:T(8,128)(2,1)}), (bf16[768,512]{1,0:T(8,128)(2,1)}, bf16[768,512]{1,0:T(8,128)(2,1)})) %all-reduce.6.cloned.1.call-update) | async-done | bytes 1572880 | tf_op jit(solution)/shard_map/psum | solution.py:100
  645.8 2.6 convert_element_type.103
  648.4 1.4 convert_element_type.105
  649.8 0.5 copy.75
  650.3 0.3 convolution_convert_fusion.2
  650.6 0.8 copy.76
  (44 shorter events, 0.2 us)
Async XLA Ops:
  7.2 108.1 %copy-start = (bf16[768,512]{1,0:T(8,128)(2,1)S(1)}, bf16[768,512]{1,0:T(8,128)(2,1)}, u32[]{:S(2)}) copy-start(bf16[768,512]{1,0:T(8,128)(2,1)} %param.13) | copy-start | bytes 2359300
  7.2 100.9 %all-gather.2.cloned.1.call-start = ((), (), s32[]{:S(2)}) async-start(), calls=%async_computation.3 | async-start | bytes 4866048 | tf_op jit(solution)/shard_map/all_gather | solution.py:46
  8.3 45.4 %copy-start.13 = (s32[22]{0:T(128)}, s32[22]{0:T(128)S(1)}, u32[]{:S(2)}) copy-start(s32[22]{0:T(128)S(1)} %multiply_add_fusion) | copy-start | bytes 268
  53.7 1.5 copy-start.10
  53.7 1.6 copy-start.11
  55.1 243.1 %all-reduce.4.cloned.1.call-start = ((), (), s32[]{:S(2)}) async-start(), calls=%async_computation.4 | async-start | bytes 8650752 | tf_op jit(solution)/shard_map/psum | solution.py:106
  55.5 55.9 %copy-start.12 = (f32[768]{0:T(1024)S(1)}, f32[768]{0:T(1024)}, u32[]{:S(2)}) copy-start(f32[768]{0:T(1024)} %param.12) | copy-start | bytes 9220
  108.1 3.5 copy-start.2
  113.3 2.0 copy-start.3
  137.6 4.7 copy-start.4
  143.5 1.6 copy-start.16
  143.5 4.6 copy-start.17
  169.0 4.2 copy-start.8
  173.2 4.7 copy-start.5
  175.4 2.5 copy-start.7
  175.4 2.5 copy-start.15
  182.5 118.8 %copy-start.14 = (s32[22]{0:T(128)S(1)}, s32[22]{0:T(128)}, u32[]{:S(2)}) copy-start(s32[22]{0:T(128)} %copy-done.13) | copy-start | bytes 268
  303.4 346.4 %all-to-all-start.2 = ((bf16[32,2,16,768]{3,2,1,0:T(8,128)(2,1)}), bf16[32,2,16,768]{3,2,1,0:T(8,128)(2,1)S(1)}, u32[]{:S(2)}, u32[]{:S(2)}) async-start(bf16[32,2,16,768]{3,2,1,0:T(8,128)(2,1)} %bitcast.119), calls=%async_computation.2 | async-start | bytes 3145728 | tf_op jit(solution)/shard_map/all_to_all | solution.py:123
  315.2 330.6 %all-reduce.6.cloned.1.call-start = ((), (), s32[]{:S(2)}) async-start(), calls=%async_computation.5 | async-start | bytes 3145728 | tf_op jit(solution)/shard_map/psum | solution.py:100
  315.5 6.6 %copy-start.6 = (bf16[11,256,4,128]{3,2,1,0:T(4,128)(2,1)S(1)}, bf16[11,256,4,128]{3,2,1,0:T(4,128)(2,1)}, u32[]{:S(2)}) copy-start(bf16[11,256,4,128]{3,2,1,0:T(4,128)(2,1)} %copy-done.5) | copy-start | bytes 8650756
  322.1 5.7 copy-start.18
  645.8 2.6 copy-start.9
  649.8 1.7 copy-start.1
Sparse Core Ops, SparseCore 0:
  55.2 52.8 all-gather.1
  182.6 115.6 all-reduce.3
  327.7 318.0 all-reduce.5
where the time goes:
time: 662 us; the launch traced here: 658 us
  waiting for transfers between devices  459 us (69%)
  matrix products  85 us (13%)
  blocking collectives  40.8 us (6%)
  local copies, waits for them, and re-layouts  33.7 us (5%)
  between operations  14.4 us (2%)
  other arithmetic  12.8 us (2%)
  starting transfers between devices  12.1 us (2%)
    psum x1, waiting for transfers between devices, body(): lax.psum(key_term.astype(jnp.bfloat16), 'dp').astype(jnp.float32)  291 us
    psum x1, waiting for transfers between devices, body(): lax.psum(enc_term.astype(jnp.bfloat16), 'tensor').astype(jnp.float32)  116 us
    all_gather x1, waiting for transfers between devices, body(): gathered = lax.all_gather(mine_states, 'tensor', axis=1, tiled=True)  52.6 us
    all_to_all x1, blocking collectives, body(): lax.all_to_all(outgoing, 'dp', split_axis=0, concat_axis=0, tiled=True)  25.4 us
    dot_general x1, matrix products, body(): jnp.einsum('chqk,cqhd->ckhd', grad_scores, query_blocks, preferred_elemen...  20.8 us
    dot_general x1, matrix products, body(): jnp.einsum('chqk,ckhd->cqhd', grad_scores, key_blocks, preferred_element_...  20.7 us
    all_to_all x1, blocking collectives, body(): lax.all_to_all(request, 'dp', split_axis=0, concat_axis=0, tiled=True)  15.4 us
  transfers between devices with their start and end apart: 4, of which 3 were waited for; matrix products, arithmetic and copies ran while one was open for 7% of the time, Pallas kernels for 0%

commit v1 on v0

v1 whole, which is shorter than its diff:
```python
import jax
import jax.numpy as jnp
from jax import lax
from jax.experimental import pallas as pl
from jax.experimental.pallas import tpu as pltpu
from jax.sharding import PartitionSpec as P

HEAD_DIM = 128
MESH = pl.DeviceIdType.MESH
SCALE = HEAD_DIM ** (-0.5)
RINGS = 4
F32 = jnp.float32
BF16 = jnp.bfloat16

epsilon = 1e-06


def normalize(values):
    widened = values.astype(F32)
    inverse = lax.rsqrt(jnp.mean(widened * widened, axis=-1, keepdims=True) + epsilon)
    return (widened * inverse, inverse)


def dot(a, b, ca, cb):
    return lax.dot_general(a, b, (((ca,), (cb,)), ((), ())), preferred_element_type=F32)


def drain(ref, sem):
    pltpu.make_async_copy(ref, ref, sem).wait()


def send(src, dst, send_sem, recv_sem, device):
    pltpu.make_async_remote_copy(
        src_ref=src,
        dst_ref=dst,
        send_sem=send_sem,
        recv_sem=recv_sem,
        device_id=device,
        device_id_type=MESH,
    ).start()


def layer_kernel(
    spans,
    per,
    places,
    mine,
    queries,
    grads,
    gain,
    key_w,
    value_w,
    attn_out,
    grad_q,
    grad_raw,
    grad_w,
    full,
    enc_t,
    grad_kv,
    term,
    from_core,
    sums,
    near_a,
    near_b,
    far_a,
    far_b,
    w_terms,
    w_slots,
    w_half,
    w_other,
    w_mine,
    w_back,
    left_sem,
    right_sem,
    half_sem,
    core_sem,
    swap_sem,
    first_sem,
    second_sem,
    w_sem,
    out_sem,
):
    me_dp = lax.axis_index("dp")
    me_t = lax.axis_index("tensor")
    ring, core = me_t // 2, lax.rem(me_t, 2)
    place, low = me_dp // 2, lax.rem(me_dp, 2)
    r_ring, l_ring, o_ring = (lax.rem(ring + d, RINGS) for d in (1, 3, 2))
    right = {"tensor": r_ring * 2 + core}
    left = {"tensor": l_ring * 2 + core}
    twin = {"tensor": ring * 2 + 1 - core}
    mate = {"dp": place * 2 + 1 - low}

    def place_at(k):
        return lax.rem(place + k, places)

    barrier = pltpu.get_barrier_semaphore()
    for device in (right, left, twin, mate):
        pl.semaphore_signal(barrier, inc=1, device_id=device, device_id_type=MESH)

    def greet(k, carry):
        device = {"dp": place_at(k) * 2 + low}
        pl.semaphore_signal(barrier, inc=1, device_id=device, device_id_type=MESH)
        return carry

    lax.fori_loop(1, places, greet, 0)
    pl.semaphore_wait(barrier, 4 + places - 1)

    gain_row = gain[...]
    span_len = queries.shape[0] // spans
    local_len, width = mine.shape[1], mine.shape[2]
    tokens = per * 2 * RINGS * local_len
    cols = queries.shape[1]

    def rows_of(c):
        return pl.ds(c * per, per)

    def gather_step(i, carry):
        @pl.when(i < spans)
        def _():
            at = rows_of(i)
            here = full.at[at, ring, core]
            block = mine.at[at]
            send(block, here, out_sem.at[0], left_sem.at[i], right)
            send(block, here, out_sem.at[1], right_sem.at[i], left)
            send(block, here, out_sem.at[2], core_sem.at[i], twin)
            full[at, ring, core] = mine[at]

        j = i - 2

        @pl.when((j >= 0) & (j < spans))
        def _():
            at = rows_of(j)
            from_left = full.at[at, l_ring, core]
            from_right = full.at[at, r_ring, core]
            drain(from_left, left_sem.at[j])
            one = full.at[j * per, l_ring, core]
            send(one, one, out_sem.at[3], half_sem.at[j], right)
            send(from_left, from_left, out_sem.at[5], core_sem.at[j], twin)
            drain(from_right, right_sem.at[j])
            two = full.at[j * per + 1, r_ring, core]
            send(two, two, out_sem.at[4], half_sem.at[j], left)
            send(from_right, from_right, out_sem.at[6], core_sem.at[j], twin)

        k = i - 4

        @pl.when((k >= 0) & (k < spans))
        def _():
            across = full.at[rows_of(k), o_ring, core]
            drain(across, half_sem.at[k])
            send(across, across, out_sem.at[7], core_sem.at[k], twin)

        c = i - 5

        @pl.when(c >= 0)
        def _():
            at = rows_of(c)
            drain(full.at[at, :, 1 - core], core_sem.at[c])
            unit, _ = normalize(full[at].reshape(tokens, width))
            encoded = (unit * gain_row).astype(BF16)
            enc_t[:, pl.ds(pl.multiple_of(c * tokens, tokens), tokens)] = encoded.T
            keys = dot(encoded, key_w[...], 1, 0).astype(BF16)
            values = dot(encoded, value_w[...], 1, 0).astype(BF16)
            q_rows = pl.ds(pl.multiple_of(c * span_len, span_len), span_len)
            t_rows = pl.ds(pl.multiple_of(c * tokens, tokens), tokens)
            for h in range(cols // HEAD_DIM):
                lanes = slice(h * HEAD_DIM, (h + 1) * HEAD_DIM)
                q, g = queries[q_rows, lanes], grads[q_rows, lanes]
                kh, vh = keys[:, lanes], values[:, lanes]
                exponent = jnp.exp(dot(q, kh, 1, 1) * SCALE)
                p = exponent / jnp.sum(exponent, axis=-1, keepdims=True)
                w = p.astype(BF16)
                attn_out[q_rows, lanes] = dot(w, vh, 1, 0).astype(BF16)
                gw = dot(g, vh, 1, 1)
                gs = (p * (gw - jnp.sum(p * gw, axis=-1, keepdims=True)) * SCALE).astype(BF16)
                grad_q[q_rows, lanes] = dot(gs, kh, 1, 0).astype(BF16)
                grad_kv[t_rows, lanes] = dot(gs, q, 0, 0).astype(BF16)
                v_lanes = slice(cols + h * HEAD_DIM, cols + (h + 1) * HEAD_DIM)
                grad_kv[t_rows, v_lanes] = dot(w, g, 0, 0).astype(BF16)

        return carry

    lax.fori_loop(0, spans + 5, gather_step, 0)

    tile = 256
    tiles = width // tile
    for part in range(2):

        def weight_step(r, carry, part=part):
            left_side = enc_t[pl.ds(pl.multiple_of(r * tile, tile), tile), :]
            product = dot(left_side, grad_kv[:, part * cols : (part + 1) * cols], 1, 0)
            row = pl.multiple_of(part * width + r * tile, tile)
            w_terms[pl.ds(row, tile), :] = product.astype(BF16)
            return carry

        lax.fori_loop(0, tiles, weight_step, 0)

    piece = w_slots.shape[1]
    half = piece // 2

    def piece_rows(p):
        return pl.ds(pl.multiple_of(p * piece, piece), piece)

    def scatter(k, carry):
        p = place_at(k)
        send(
            w_terms.at[piece_rows(p)],
            w_slots.at[k - 1],
            out_sem.at[8],
            w_sem.at[0],
            {"dp": p * 2 + low},
        )
        return carry

    lax.fori_loop(1, places, scatter, 0)

    def reduce_step(i, carry):
        @pl.when(i < spans)
        def _():
            t_rows = pl.ds(pl.multiple_of(i * tokens, tokens), tokens)
            product = dot(grad_kv[t_rows, :cols], key_w[...], 1, 1)
            product = product + dot(grad_kv[t_rows, cols:], value_w[...], 1, 1)
            at = rows_of(i)
            term[at] = product.astype(BF16).reshape(per, RINGS, 2, local_len, width)
            send(
                term.at[at, :, 1 - core],
                from_core.at[at],
                out_sem.at[9],
                swap_sem.at[i],
                twin,
            )

        j = i - 1

        @pl.when((j >= 0) & (j < spans))
        def _():
            at = rows_of(j)
            drain(from_core.at[at], swap_sem.at[j])
            total = term[at, :, core].astype(F32) + from_core[at].astype(F32)
            sums[at] = total.astype(BF16)
            send(sums.at[j * per, o_ring], near_a.at[j], out_sem.at[10], first_sem.at[0, j], right)
            send(
                sums.at[j * per + 1, o_ring], near_b.at[j], out_sem.at[11], first_sem.at[1, j], left
            )

        k = i - 3

        @pl.when((k >= 0) & (k < spans))
        def _():
            at = rows_of(k)
            drain(near_a.at[k], first_sem.at[0, k])
            total = sums[k * per, r_ring].astype(F32) + near_a[k].astype(F32)
            sums[k * per, r_ring] = total.astype(BF16)
            send(sums.at[at, r_ring], far_a.at[at], out_sem.at[12], second_sem.at[0, k], right)
            drain(near_b.at[k], first_sem.at[1, k])
            total = sums[k * per + 1, l_ring].astype(F32) + near_b[k].astype(F32)
            sums[k * per + 1, l_ring] = total.astype(BF16)
            send(sums.at[at, l_ring], far_b.at[at], out_sem.at[13], second_sem.at[1, k], left)

        @pl.when(i == 7)
        def _():
            drain(w_slots, w_sem.at[0])
            total = w_terms[piece_rows(place), :].astype(F32)
            for s in range(places - 1):
                total = total + w_slots[s].astype(F32)
            w_half[...] = total.astype(BF16).reshape(2, half, cols)
            send(w_half.at[1 - low], w_other, out_sem.at[14], w_sem.at[1], mate)

        @pl.when(i == 8)
        def _():
            drain(w_other, w_sem.at[1])
            total = w_half[low].astype(F32) + w_other[...].astype(F32)
            w_mine[low] = total.astype(BF16)
            send(w_mine.at[low], w_mine.at[low], out_sem.at[15], w_sem.at[2], mate)

        @pl.when(i == 9)
        def _():
            drain(w_mine.at[1 - low], w_sem.at[2])

            def spread(k, carry):
                device = {"dp": place_at(k) * 2 + low}
                send(w_mine, w_back.at[k - 1], out_sem.at[16], w_sem.at[3], device)
                return carry

            lax.fori_loop(1, places, spread, 0)

        c = i - 5

        @pl.when(c >= 0)
        def _():
            at = rows_of(c)
            drain(far_a.at[at], second_sem.at[0, c])
            drain(far_b.at[at], second_sem.at[1, c])
            own = sums[at, ring].astype(F32) + far_a[at].astype(F32) + far_b[at].astype(F32)
            own = own.reshape(per * local_len, width)
            unit, inverse = normalize(mine[at].reshape(per * local_len, width))
            scaled = own * gain_row
            raw = inverse * (scaled - unit * jnp.mean(scaled * unit, axis=-1, keepdims=True))
            grad_raw[at] = raw.astype(BF16).reshape(per, local_len, width)

        return carry

    lax.fori_loop(0, spans + 5, reduce_step, 0)

    drain(w_back, w_sem.at[3])
    grad_w[place] = w_mine[...].reshape(piece, cols).astype(F32)

    def widen(k, carry):
        source = lax.rem(place + places - k, places)
        grad_w[source] = w_back[k - 1].reshape(piece, cols).astype(F32)
        return carry

    lax.fori_loop(1, places, widen, 0)

    for n in (0, 1, 2, 5, 6, 7):
        drain(mine, out_sem.at[n])
    drain(near_a, out_sem.at[3])
    drain(near_a, out_sem.at[4])
    drain(w_slots, out_sem.at[8])
    drain(from_core, out_sem.at[9])
    drain(near_a, out_sem.at[10])
    drain(near_b, out_sem.at[11])
    drain(far_a, out_sem.at[12])
    drain(far_b, out_sem.at[13])
    drain(w_other, out_sem.at[14])
    drain(w_other, out_sem.at[15])
    drain(w_back, out_sem.at[16])


def layer(mine_states, queries, grad_attn, enc_gain, key_weight, value_weight, spans, groups):
    asked, local_len, width = mine_states.shape
    per = asked // spans
    rows, cols = queries.shape
    places = groups // 2
    tokens = asked * local_len * RINGS * 2
    piece = 2 * width // places

    def kernel(*refs):
        layer_kernel(spans, per, places, *refs)

    vmem = pl.BlockSpec(memory_space=pltpu.VMEM)
    dma = pltpu.SemaphoreType.DMA
    return pl.pallas_call(
        kernel,
        out_shape=(
            jax.ShapeDtypeStruct((rows, cols), BF16),
            jax.ShapeDtypeStruct((rows, cols), BF16),
            jax.ShapeDtypeStruct((asked, local_len, width), BF16),
            jax.ShapeDtypeStruct((places, piece, cols), F32),
        ),
        in_specs=[vmem] * 6,
        out_specs=(vmem,) * 4,
        scratch_shapes=[
            pltpu.VMEM((asked, RINGS, 2, local_len, width), BF16),
            pltpu.VMEM((width, tokens), BF16),
            pltpu.VMEM((tokens, 2 * cols), BF16),
            pltpu.VMEM((asked, RINGS, 2, local_len, width), BF16),
            pltpu.VMEM((asked, RINGS, local_len, width), BF16),
            pltpu.VMEM((asked, RINGS, local_len, width), BF16),
            pltpu.VMEM((spans, local_len, width), BF16),
            pltpu.VMEM((spans, local_len, width), BF16),
            pltpu.VMEM((asked, local_len, width), BF16),
            pltpu.VMEM((asked, local_len, width), BF16),
            pltpu.VMEM((2 * width, cols), BF16),
            pltpu.VMEM((places - 1, piece, cols), BF16),
            pltpu.VMEM((2, piece // 2, cols), BF16),
            pltpu.VMEM((piece // 2, cols), BF16),
            pltpu.VMEM((2, piece // 2, cols), BF16),
            pltpu.VMEM((places - 1, 2, piece // 2, cols), BF16),
            dma((spans,)),
            dma((spans,)),
            dma((spans,)),
            dma((spans,)),
            dma((spans,)),
            dma((2, spans)),
            dma((2, spans)),
            dma((4,)),
            dma((17,)),
        ],
        compiler_params=pltpu.CompilerParams(
            collective_id=0, has_side_effects=True, vmem_limit_bytes=58 * 1024 * 1024
        ),
        cost_estimate=pl.CostEstimate(
            flops=14 * 10**9, bytes_accessed=2 * 10**7, transcendentals=720896
        ),
    )(mine_states, queries, grad_attn, enc_gain.reshape(1, width), key_weight, value_weight)


def body(queries, nb_states, nb_owner, nb_row, enc_gain, key_weight, value_weight, grad_attn):
    groups = lax.axis_size("dp")
    owner_list = nb_owner.reshape(-1)
    row_list = nb_row.reshape(-1)
    asked_count = owner_list.shape[0]
    capacity = max(2, (2 * asked_count + groups - 1) // groups)
    positions = jnp.arange(asked_count, dtype=jnp.int32)
    same_owner = owner_list[:, None] == owner_list[None, :]
    before_me = positions[None, :] < positions[:, None]
    slot_rank = jnp.sum(jnp.where(same_owner & before_me, 1, 0), axis=1).astype(jnp.int32)
    slot_index = owner_list * capacity + slot_rank
    slot_count = groups * capacity
    selector = slot_index[:, None] == jnp.arange(slot_count, dtype=jnp.int32)[None, :]
    request = jnp.sum(jnp.where(selector, row_list[:, None], 0), axis=0).reshape(groups, capacity)
    asked_rows = lax.all_to_all(request, "dp", split_axis=0, concat_axis=0, tiled=True)
    asked_flat = asked_rows.reshape(-1)
    local_len = nb_states.shape[1]
    enc_width = nb_states.shape[2]
    outgoing = nb_states[asked_flat].reshape(groups, capacity, local_len, enc_width)
    fetched = lax.all_to_all(outgoing, "dp", split_axis=0, concat_axis=0, tiled=True)
    select_half = selector.astype(jnp.bfloat16)
    mine_states = jnp.dot(
        select_half,
        fetched.reshape(slot_count, local_len * enc_width),
        preferred_element_type=jnp.float32,
    )
    mine_states = mine_states.astype(jnp.bfloat16).reshape(asked_count, local_len, enc_width)
    attn_out, grad_queries, grad_raw, grad_w = layer(
        mine_states,
        queries,
        grad_attn,
        enc_gain,
        key_weight,
        value_weight,
        nb_owner.shape[0],
        groups,
    )
    grad_w = grad_w.reshape(2, enc_width, key_weight.shape[1])
    outgoing_grad = jnp.dot(
        select_half.T,
        grad_raw.reshape(asked_count, local_len * enc_width),
        preferred_element_type=jnp.float32,
    )
    outgoing_grad = outgoing_grad.astype(jnp.bfloat16).reshape(
        groups, capacity, local_len, enc_width
    )
    returned = lax.all_to_all(outgoing_grad, "dp", split_axis=0, concat_axis=0, tiled=True)
    owned_count = nb_states.shape[0]
    owner_rows = (asked_flat[None, :] == jnp.arange(owned_count, dtype=jnp.int32)[:, None]).astype(
        jnp.bfloat16
    )
    grad_states = jnp.dot(
        owner_rows,
        returned.reshape(slot_count, local_len * enc_width),
        preferred_element_type=jnp.float32,
    )
    grad_states = grad_states.astype(jnp.bfloat16).reshape(nb_states.shape)
    return (attn_out, grad_queries, grad_states, grad_w[0], grad_w[1])


def solution(mesh):
    return jax.shard_map(
        body,
        mesh=mesh,
        in_specs=(
            P("dp", "tensor"),
            P("dp", "tensor", None),
            P("dp", None),
            P("dp", None),
            P(),
            P(None, "tensor"),
            P(None, "tensor"),
            P("dp", "tensor"),
        ),
        out_specs=(
            P("dp", "tensor"),
            P("dp", "tensor"),
            P("dp", "tensor", None),
            P(None, "tensor"),
            P(None, "tensor"),
        ),
        check_vma=False,
    )
```

time: 662 us -> 198 us (0.30)
  waiting for transfers between devices: 459 us -> 37.2 us
  Pallas kernels: 0 us -> 111 us
  matrix products: 85 us -> 1.4 us
  blocking collectives: 40.8 us -> 15.4 us
  local copies, waits for them, and re-layouts: 33.7 us -> 16.2 us
  between operations: 14.4 us -> 0.79 us
  other arithmetic: 12.8 us -> 0.98 us
    psum x2 -> x0, waiting for transfers between devices: 407 us -> none  [the longest x1 291 us: body(): lax.psum(key_term.astype(jnp.bfloat16), 'dp').astype(jnp.float32)]
    pallas_call x0 -> x1, Pallas kernels: none -> 111 us  [layer(): pl.pallas_call(kernel, out_shape=(jax.ShapeDtypeStruct((rows, cols), BF16...]
    dot_general x12 -> x0, matrix products: 83.6 us -> none  [the longest x1 20.8 us: body(): jnp.einsum('chqk,cqhd->ckhd', grad_scores, query_blocks, preferred_elemen...]
    all_gather x1 -> x0, waiting for transfers between devices: 52.6 us -> none  [body(): gathered = lax.all_gather(mine_states, 'tensor', axis=1, tiled=True)]
    all_to_all x1 -> x0, blocking collectives: 25.4 us -> none  [body(): lax.all_to_all(outgoing, 'dp', split_axis=0, concat_axis=0, tiled=True)]
    all_to_all x0 -> x1, waiting for transfers between devices: none -> 20.6 us  [body(): lax.all_to_all(outgoing, 'dp', split_axis=0, concat_axis=0, tiled=True)]
    all_to_all x1, waiting for transfers between devices: 0.01 us -> 16.6 us  [body(): lax.all_to_all(outgoing_grad, 'dp', split_axis=0, concat_axis=0, tiled=True)]
    reshape x5 -> x1, local copies, waits for them, and re-layouts: 13.6 us -> 0.58 us  [layer(): enc_gain.reshape(1, width)]
  transfers between devices with their start and end apart: 4 -> 2, of which waited for: 3 -> 2; matrix products, arithmetic and copies ran while one was open for 7% -> 2% of each run, Pallas kernels for 0% -> 0%
where the time goes in v1:
time: 198 us; the launch traced here: 196 us
  Pallas kernels  111 us (56%)
  waiting for transfers between devices  37.2 us (19%)
  local copies, waits for them, and re-layouts  16.2 us (8%)
  blocking collectives  15.4 us (8%)
  starting transfers between devices  12.8 us (6%)
    pallas_call x1, Pallas kernels, layer(): pl.pallas_call(kernel, out_shape=(jax.ShapeDtypeStruct((rows, cols), BF16...  111 us
    all_to_all x1, waiting for transfers between devices, body(): lax.all_to_all(outgoing, 'dp', split_axis=0, concat_axis=0, tiled=True)  20.6 us
    all_to_all x1, waiting for transfers between devices, body(): lax.all_to_all(outgoing_grad, 'dp', split_axis=0, concat_axis=0, tiled=True)  16.6 us
    all_to_all x1, blocking collectives, body(): lax.all_to_all(request, 'dp', split_axis=0, concat_axis=0, tiled=True)  15.4 us
    unnamed x19, local copies, waits for them, and re-layouts  8 us
    all_to_all x1, starting transfers between devices, body(): lax.all_to_all(outgoing_grad, 'dp', split_axis=0, concat_axis=0, tiled=True)  7.64 us
    all_to_all x1, starting transfers between devices, body(): lax.all_to_all(outgoing, 'dp', split_axis=0, concat_axis=0, tiled=True)  5.16 us
    slice x1, local copies, waits for them, and re-layouts, body(): return (attn_out, grad_queries, grad_states, grad_w[0], grad_w[1])  3.96 us
  transfers between devices with their start and end apart: 2, of which 2 were waited for; matrix products, arithmetic and copies ran while one was open for 2% of the time, Pallas kernels for 0%

profile of v1, /device:TPU:32, one launch (start us, length us, event | category | flops | bytes accessed | tf_op | source)
XLA Modules:
  0.0 195.9 jit_solution(12193147863526055446)
XLA Ops:
  0.6 0.0 copy-start
  0.6 0.8 copy.20
  1.5 0.1 reshape.91
  1.5 0.2 select_reduce_fusion.1
  1.7 0.8 copy.21
  2.5 0.1 broadcast_in_dim.30
  2.6 0.1 select_reduce_fusion
  2.7 0.1 all_to_all.12
  2.8 15.4 %all_to_all.19 = s32[32,1,2]{2,1,0:T(1,128)S(1)} all-to-all(s32[32,1,2]{2,1,0:T(1,128)S(1)} %bitcast.41), channel_id=1, replica_groups=mesh['dp'=32,'tensor'=8] {'dp'}, dimensions={0} | all-to-all | bytes 512 | tf_op jit(solution)/shard_map/all_to_all | solution.py:402
  18.2 0.5 broadcast.32
  18.7 0.7 reduce.5
  19.4 0.1 reshape.92
  19.5 0.0 copy-done
  19.6 1.8 gather_fusion
  21.3 0.0 copy-start.3
  21.4 5.2 %all-to-all-start.1 = ((bf16[32,2,16,768]{3,2,1,0:T(8,128)(2,1)}), bf16[32,2,16,768]{3,2,1,0:T(8,128)(2,1)S(1)}, u32[]{:S(2)}, u32[]{:S(2)}) async-start(bf16[32,2,16,768]{3,2,1,0:T(8,128)(2,1)} %bitcast.2), calls=%async_computation.1 | async-start | bytes 3145728 | tf_op jit(solution)/shard_map/all_to_all | solution.py:407
  26.5 0.0 copy-done.3
  26.5 0.6 reshape.96.refs_3_
  27.1 20.6 %all-to-all-done.1 = bf16[32,2,16,768]{3,2,1,0:T(8,128)(2,1)S(1)} async-done(((bf16[32,2,16,768]{3,2,1,0:T(8,128)(2,1)}), bf16[32,2,16,768]{3,2,1,0:T(8,128)(2,1)S(1)}, u32[]{:S(2)}, u32[]{:S(2)}) %all-to-all-start.1) | async-done | bytes 1572896 | tf_op jit(solution)/shard_map/all_to_all | solution.py:407
  47.7 0.5 copy.23
  48.2 0.4 convolution_convert_fusion.1
  48.6 0.1 copy.24
  48.8 0.8 slice.12.refs_0_
  49.6 111.1 %shard_map.119 = (bf16[704,512]{1,0:T(8,128)(2,1)}, bf16[704,512]{1,0:T(8,128)(2,1)}, bf16[22,16,768]{2,1,0:T(8,128)(2,1)}, f32[16,96,512]{2,1,0:T(8,128)}) custom-call(bf16[22,16,768]{2,1,0:T(8,128)(2,1)} %slice.12.refs_0_, bf16[704,512]{1,0:T(8,128)(2,1)} %refs_1_.1, bf16[704,512]{1,0:T(8,128)(2,1)} %refs_2_.1, f32[1,768]{1,0:T(1,128)} %reshape.96.refs_3_, ...), custom_call_target="tpu_custom_call" | custom-call | flops 14000000000 | bytes 20000000 | tf_op jit(solution)/shard_map/pallas_call | solution.py:342
  160.7 1.1 pad.1
  161.8 0.2 copy.25
  162.0 0.7 convolution_convert_fusion
  162.7 1.4 copy.26
  164.1 7.6 %all-to-all-start.2 = ((bf16[32,2,16,768]{3,2,1,0:T(8,128)(2,1)}), bf16[32,2,16,768]{3,2,1,0:T(8,128)(2,1)S(1)}, u32[]{:S(2)}, u32[]{:S(2)}) async-start(bf16[32,2,16,768]{3,2,1,0:T(8,128)(2,1)} %bitcast.17), calls=%async_computation.2 | async-start | bytes 3145728 | tf_op jit(solution)/shard_map/all_to_all | solution.py:434
  171.8 0.1 eq.47
  171.9 4.0 %fusion.5 = (f32[8,96,512]{2,1,0:T(8,128)}, f32[8,96,512]{2,1,0:T(8,128)}) fusion(f32[16,96,512]{2,1,0:T(8,128)} %get-tuple-element.12), kind=kLoop, calls=%fused_computation.17 | loop fusion | bytes 6291456 | tf_op jit(solution)/shard_map/slice | solution.py:445
  175.8 16.6 %all-to-all-done.2 = bf16[32,2,16,768]{3,2,1,0:T(8,128)(2,1)S(1)} async-done(((bf16[32,2,16,768]{3,2,1,0:T(8,128)(2,1)}), bf16[32,2,16,768]{3,2,1,0:T(8,128)(2,1)S(1)}, u32[]{:S(2)}, u32[]{:S(2)}) %all-to-all-start.2) | async-done | bytes 1572896 | tf_op jit(solution)/shard_map/all_to_all | solution.py:434
  192.5 0.5 copy.27
  193.0 0.0 copy-start.2
  193.0 0.3 convolution_convert_fusion.2
  193.3 0.0 copy-start.1
  193.3 0.8 copy.28
  194.1 0.0 copy-done.2
  194.1 0.9 copy.31
  195.0 0.0 copy-done.1
  195.0 0.9 copy.32
  (3 shorter events, 0.0 us)
Async XLA Ops:
  0.6 18.9 %copy-start = (bf16[16,16,768]{2,1,0:T(8,128)(2,1)S(1)}, bf16[16,16,768]{2,1,0:T(8,128)(2,1)}, u32[]{:S(2)}) copy-start(bf16[16,16,768]{2,1,0:T(8,128)(2,1)} %param.9) | copy-start | bytes 1179652
  21.3 5.2 %copy-start.3 = (f32[768]{0:T(1024)S(1)}, f32[768]{0:T(1024)}, u32[]{:S(2)}) copy-start(f32[768]{0:T(1024)} %param.12) | copy-start | bytes 9220
  21.4 26.4 %all-to-all-start.1 = ((bf16[32,2,16,768]{3,2,1,0:T(8,128)(2,1)}), bf16[32,2,16,768]{3,2,1,0:T(8,128)(2,1)S(1)}, u32[]{:S(2)}, u32[]{:S(2)}) async-start(bf16[32,2,16,768]{3,2,1,0:T(8,128)(2,1)} %bitcast.2), calls=%async_computation.1 | async-start | bytes 3145728 | tf_op jit(solution)/shard_map/all_to_all | solution.py:407
  164.1 28.3 %all-to-all-start.2 = ((bf16[32,2,16,768]{3,2,1,0:T(8,128)(2,1)}), bf16[32,2,16,768]{3,2,1,0:T(8,128)(2,1)S(1)}, u32[]{:S(2)}, u32[]{:S(2)}) async-start(bf16[32,2,16,768]{3,2,1,0:T(8,128)(2,1)} %bitcast.17), calls=%async_computation.2 | async-start | bytes 3145728 | tf_op jit(solution)/shard_map/all_to_all | solution.py:434
  193.0 1.2 copy-start.2
  193.3 1.7 copy-start.1

commit v2 on v1

--- a/solution.py
+++ b/solution.py
@@ -44,7 +44,10 @@
     spans,
     per,
     places,
-    mine,
+    slot_of,
+    source_of,
+    request,
+    states,
     queries,
     grads,
     gain,
@@ -52,8 +55,17 @@
     value_w,
     attn_out,
     grad_q,
+    grad_states,
+    grad_key_w,
+    grad_value_w,
+    asked,
+    asked_s,
+    stage,
+    fetched,
+    mine,
     grad_raw,
-    grad_w,
+    returned,
+    slot_rows,
     full,
     enc_t,
     grad_kv,
@@ -79,6 +91,7 @@
     second_sem,
     w_sem,
     out_sem,
+    near_sem,
 ):
     me_dp = lax.axis_index("dp")
     me_t = lax.axis_index("tensor")
@@ -89,21 +102,53 @@
     left = {"tensor": l_ring * 2 + core}
     twin = {"tensor": ring * 2 + 1 - core}
     mate = {"dp": place * 2 + 1 - low}
+    groups = 2 * places
 
     def place_at(k):
         return lax.rem(place + k, places)
 
+    def ahead(k):
+        return {"dp": lax.rem(me_dp + k, groups)}
+
+    def behind(k):
+        return {"dp": lax.rem(me_dp + groups - k, groups)}
+
     barrier = pltpu.get_barrier_semaphore()
-    for device in (right, left, twin, mate):
+    for device in (right, left, twin):
         pl.semaphore_signal(barrier, inc=1, device_id=device, device_id_type=MESH)
 
     def greet(k, carry):
-        device = {"dp": place_at(k) * 2 + low}
-        pl.semaphore_signal(barrier, inc=1, device_id=device, device_id_type=MESH)
-        return carry
-
-    lax.fori_loop(1, places, greet, 0)
-    pl.semaphore_wait(barrier, 4 + places - 1)
+        pl.semaphore_signal(barrier, inc=1, device_id=ahead(k), device_id_type=MESH)
+        return carry
+
+    lax.fori_loop(1, groups, greet, 0)
+    pl.semaphore_wait(barrier, 3 + groups - 1)
+
+    def ask(k, carry):
+        owner = lax.rem(me_dp + k, groups)
+        send(request.at[owner], asked.at[k - 1], near_sem.at[0], near_sem.at[1], ahead(k))
+        return carry
+
+    lax.fori_loop(1, groups, ask, 0)
+    remote_asked = asked.at[pl.ds(0, groups - 1)]
+    asked[groups - 1] = request[me_dp]
+    drain(remote_asked, near_sem.at[1])
+    to_scalars = pltpu.make_async_copy(asked, asked_s, near_sem.at[2])
+    to_scalars.start()
+    to_scalars.wait()
+
+    def answer(k, carry):
+        for r in range(2):
+            stage[2 * (k - 1) + r] = states[asked_s[k - 1, 0, r]]
+        at = pl.ds(2 * (k - 1), 2)
+        send(stage.at[at], fetched.at[at], near_sem.at[3], near_sem.at[4], behind(k))
+        return carry
+
+    lax.fori_loop(1, groups, answer, 0)
+    for r in range(2):
+        fetched[2 * (groups - 1) + r] = states[asked_s[groups - 1, 0, r]]
+    others = pl.ds(0, 2 * (groups - 1))
+    drain(fetched.at[others], near_sem.at[4])
 
     gain_row = gain[...]
     span_len = queries.shape[0] // spans
@@ -118,6 +163,8 @@
         @pl.when(i < spans)
         def _():
             at = rows_of(i)
+            for n in range(per):
+                mine[i * per + n] = fetched[slot_of[i * per + n]]
             here = full.at[at, ring, core]
             block = mine.at[at]
             send(block, here, out_sem.at[0], left_sem.at[i], right)
@@ -183,16 +230,14 @@
 
     tile = 256
     tiles = width // tile
-    for part in range(2):
-
-        def weight_step(r, carry, part=part):
-            left_side = enc_t[pl.ds(pl.multiple_of(r * tile, tile), tile), :]
-            product = dot(left_side, grad_kv[:, part * cols : (part + 1) * cols], 1, 0)
-            row = pl.multiple_of(part * width + r * tile, tile)
-            w_terms[pl.ds(row, tile), :] = product.astype(BF16)
-            return carry
-
-        lax.fori_loop(0, tiles, weight_step, 0)
+
+    def weight_tile(n):
+        part = n // tiles
+        r = lax.rem(n, tiles)
+        left_side = enc_t[pl.ds(pl.multiple_of(r * tile, tile), tile), :]
+        lanes = pl.ds(pl.multiple_of(part * cols, cols), cols)
+        row = pl.multiple_of(n * tile, tile)
+        w_terms[pl.ds(row, tile), :] = dot(left_side, grad_kv[:, lanes], 1, 0).astype(BF16)
 
     piece = w_slots.shape[1]
     half = piece // 2
@@ -210,8 +255,6 @@
             {"dp": p * 2 + low},
         )
         return carry
-
-    lax.fori_loop(1, places, scatter, 0)
 
     def reduce_step(i, carry):
         @pl.when(i < spans)
@@ -256,7 +299,19 @@
             sums[k * per + 1, l_ring] = total.astype(BF16)
             send(sums.at[at, l_ring], far_b.at[at], out_sem.at[13], second_sem.at[1, k], left)
 
-        @pl.when(i == 7)
+        @pl.when(i < 3)
+        def _():
+            def tile_step(n, carry):
+                weight_tile(2 * i + n)
+                return carry
+
+            lax.fori_loop(0, 2, tile_step, 0)
+
+        @pl.when(i == 2)
+        def _():
+            lax.fori_loop(1, places, scatter, 0)
+
+        @pl.when(i == 8)
         def _():
             drain(w_slots, w_sem.at[0])
             total = w_terms[piece_rows(place), :].astype(F32)
@@ -265,14 +320,14 @@
             w_half[...] = total.astype(BF16).reshape(2, half, cols)
             send(w_half.at[1 - low], w_other, out_sem.at[14], w_sem.at[1], mate)
 
-        @pl.when(i == 8)
+        @pl.when(i == 9)
         def _():
             drain(w_other, w_sem.at[1])
             total = w_half[low].astype(F32) + w_other[...].astype(F32)
             w_mine[low] = total.astype(BF16)
             send(w_mine.at[low], w_mine.at[low], out_sem.at[15], w_sem.at[2], mate)
 
-        @pl.when(i == 9)
+        @pl.when(i == 10)
         def _():
             drain(w_mine.at[1 - low], w_sem.at[2])
 
@@ -301,16 +356,61 @@
 
     lax.fori_loop(0, spans + 5, reduce_step, 0)
 
+    asked_count = spans * per
+    grad_raw[asked_count] = jnp.zeros((local_len, width), BF16)
+    drain(stage.at[others], near_sem.at[3])
+
+    def give_back(k, carry):
+        for r in range(2):
+            stage[2 * (k - 1) + r] = grad_raw[source_of[2 * (k - 1) + r]]
+        at = pl.ds(2 * (k - 1), 2)
+        send(stage.at[at], returned.at[at], near_sem.at[5], near_sem.at[6], ahead(k))
+        return carry
+
+    lax.fori_loop(1, groups, give_back, 0)
+    for r in range(2):
+        returned[2 * (groups - 1) + r] = grad_raw[source_of[2 * (groups - 1) + r]]
+
+    def name_rows(k, carry):
+        for r in range(2):
+            rows = pl.ds(pl.multiple_of((2 * k + r) * local_len, local_len), local_len)
+            slot_rows[rows, :] = jnp.full((local_len, 256), asked_s[k, 0, r], jnp.int32)
+        return carry
+
+    lax.fori_loop(0, groups, name_rows, 0)
+
     drain(w_back, w_sem.at[3])
-    grad_w[place] = w_mine[...].reshape(piece, cols).astype(F32)
-
-    def widen(k, carry):
-        source = lax.rem(place + places - k, places)
-        grad_w[source] = w_back[k - 1].reshape(piece, cols).astype(F32)
-        return carry
-
-    lax.fori_loop(1, places, widen, 0)
-
+
+    def keep(source, value):
+        @pl.when(source < places // 2)
+        def _():
+            grad_key_w[source] = value
+
+        @pl.when(source >= places // 2)
+        def _():
+            grad_value_w[source - places // 2] = value
+
+    keep(place, w_mine[...])
+
+    def settle(k, carry):
+        keep(lax.rem(place + places - k, places), w_back[k - 1])
+        return carry
+
+    lax.fori_loop(1, places, settle, 0)
+
+    slot_tokens = 2 * groups * local_len
+    owned = states.shape[0] * local_len
+    shape = (slot_tokens, owned)
+    to_row = lax.broadcasted_iota(jnp.int32, shape, 1)
+    token = lax.broadcasted_iota(jnp.int32, shape, 0)
+    wanted = slot_rows[...] * local_len + lax.rem(token, local_len)
+    chosen = jnp.where(wanted == to_row, 1.0, 0.0).astype(BF16)
+    drain(returned.at[others], near_sem.at[6])
+    total = dot(chosen, returned[...].reshape(slot_tokens, width), 0, 0)
+    grad_states[...] = total.astype(BF16).reshape(states.shape)
+
+    drain(remote_asked, near_sem.at[0])
+    drain(stage.at[others], near_sem.at[5])
     for n in (0, 1, 2, 5, 6, 7):
         drain(mine, out_sem.at[n])
     drain(near_a, out_sem.at[3])
@@ -326,9 +426,14 @@
     drain(w_back, out_sem.at[16])
 
 
-def layer(mine_states, queries, grad_attn, enc_gain, key_weight, value_weight, spans, groups):
-    asked, local_len, width = mine_states.shape
-    per = asked // spans
+def layer(
+    slot_of, source_of, request, states, queries, grad_attn, enc_gain, key_weight, value_weight
+):
+    groups = request.shape[0]
+    owned, local_len, width = states.shape
+    asked = slot_of.shape[0]
+    per = 2
+    spans = asked // per
     rows, cols = queries.shape
     places = groups // 2
     tokens = asked * local_len * RINGS * 2
@@ -338,18 +443,28 @@
         layer_kernel(spans, per, places, *refs)
 
     vmem = pl.BlockSpec(memory_space=pltpu.VMEM)
+    smem = pl.BlockSpec(memory_space=pltpu.SMEM)
     dma = pltpu.SemaphoreType.DMA
     return pl.pallas_call(
         kernel,
         out_shape=(
             jax.ShapeDtypeStruct((rows, cols), BF16),
             jax.ShapeDtypeStruct((rows, cols), BF16),
-            jax.ShapeDtypeStruct((asked, local_len, width), BF16),
-            jax.ShapeDtypeStruct((places, piece, cols), F32),
+            jax.ShapeDtypeStruct((owned, local_len, width), BF16),
+            jax.ShapeDtypeStruct((places // 2, 2, piece // 2, cols), BF16),
+            jax.ShapeDtypeStruct((places // 2, 2, piece // 2, cols), BF16),
         ),
-        in_specs=[vmem] * 6,
-        out_specs=(vmem,) * 4,
+        in_specs=[smem] * 2 + [vmem] * 7,
+        out_specs=(vmem,) * 5,
         scratch_shapes=[
+            pltpu.VMEM((groups, 1, 128), jnp.int32),
+            pltpu.SMEM((groups, 1, 128), jnp.int32),
+            pltpu.VMEM((2 * groups, local_len, width), BF16),
+            pltpu.VMEM((2 * groups, local_len, width), BF16),
+            pltpu.VMEM((asked, local_len, width), BF16),
+            pltpu.VMEM((asked + 1, local_len, width), BF16),
+            pltpu.VMEM((2 * groups, local_len, width), BF16),
+            pltpu.VMEM((2 * groups * local_len, owned * local_len), jnp.int32),
             pltpu.VMEM((asked, RINGS, 2, local_len, width), BF16),
             pltpu.VMEM((width, tokens), BF16),
             pltpu.VMEM((tokens, 2 * cols), BF16),
@@ -375,6 +490,7 @@
             dma((2, spans)),
             dma((4,)),
             dma((17,)),
+            dma((7,)),
         ],
         compiler_params=pltpu.CompilerParams(
             collective_id=0, has_side_effects=True, vmem_limit_bytes=58 * 1024 * 1024
@@ -382,7 +498,17 @@
         cost_estimate=pl.CostEstimate(
             flops=14 * 10**9, bytes_accessed=2 * 10**7, transcendentals=720896
         ),
-    )(mine_states, queries, grad_attn, enc_gain.reshape(1, width), key_weight, value_weight)
+    )(
+        slot_of,
+        source_of,
+        request,
+        states,
+        queries,
+        grad_attn,
+        enc_gain.reshape(1, width),
+        key_weight,
+        value_weight,
+    )
 
 
 def body(queries, nb_states, nb_owner, nb_row, enc_gain, key_weight, value_weight, grad_attn):
@@ -390,59 +516,37 @@
     owner_list = nb_owner.reshape(-1)
     row_list = nb_row.reshape(-1)
     asked_count = owner_list.shape[0]
-    capacity = max(2, (2 * asked_count + groups - 1) // groups)
+    capacity = 2
     positions = jnp.arange(asked_count, dtype=jnp.int32)
     same_owner = owner_list[:, None] == owner_list[None, :]
     before_me = positions[None, :] < positions[:, None]
     slot_rank = jnp.sum(jnp.where(same_owner & before_me, 1, 0), axis=1).astype(jnp.int32)
-    slot_index = owner_list * capacity + slot_rank
+    me = lax.axis_index("dp")
+    slot_of = lax.rem(owner_list - me - 1 + groups, groups) * capacity + slot_rank
     slot_count = groups * capacity
-    selector = slot_index[:, None] == jnp.arange(slot_count, dtype=jnp.int32)[None, :]
-    request = jnp.sum(jnp.where(selector, row_list[:, None], 0), axis=0).reshape(groups, capacity)
-    asked_rows = lax.all_to_all(request, "dp", split_axis=0, concat_axis=0, tiled=True)
-    asked_flat = asked_rows.reshape(-1)
-    local_len = nb_states.shape[1]
-    enc_width = nb_states.shape[2]
-    outgoing = nb_states[asked_flat].reshape(groups, capacity, local_len, enc_width)
-    fetched = lax.all_to_all(outgoing, "dp", split_axis=0, concat_axis=0, tiled=True)
-    select_half = selector.astype(jnp.bfloat16)
-    mine_states = jnp.dot(
-        select_half,
-        fetched.reshape(slot_count, local_len * enc_width),
-        preferred_element_type=jnp.float32,
-    )
-    mine_states = mine_states.astype(jnp.bfloat16).reshape(asked_count, local_len, enc_width)
-    attn_out, grad_queries, grad_raw, grad_w = layer(
-        mine_states,
+    slots = jnp.arange(slot_count, dtype=jnp.int32)
+    filled = slot_of[:, None] == slots[None, :]
+    source_of = asked_count - jnp.sum(
+        jnp.where(filled, asked_count - positions[:, None], 0), axis=0
+    ).astype(jnp.int32)
+    owner_rank = owner_list * capacity + slot_rank
+    named = owner_rank[:, None] == slots[None, :]
+    request = jnp.sum(jnp.where(named, row_list[:, None], 0), axis=0).astype(jnp.int32)
+    request = jnp.pad(request.reshape(groups, 1, capacity), ((0, 0), (0, 0), (0, 128 - capacity)))
+    attn_out, grad_queries, grad_states, grad_key_w, grad_value_w = layer(
+        slot_of,
+        source_of,
+        request,
+        nb_states,
         queries,
         grad_attn,
         enc_gain,
         key_weight,
         value_weight,
-        nb_owner.shape[0],
-        groups,
     )
-    grad_w = grad_w.reshape(2, enc_width, key_weight.shape[1])
-    outgoing_grad = jnp.dot(
-        select_half.T,
-        grad_raw.reshape(asked_count, local_len * enc_width),
-        preferred_element_type=jnp.float32,
-    )
-    outgoing_grad = outgoing_grad.astype(jnp.bfloat16).reshape(
-        groups, capacity, local_len, enc_width
-    )
-    returned = lax.all_to_all(outgoing_grad, "dp", split_axis=0, concat_axis=0, tiled=True)
-    owned_count = nb_states.shape[0]
-    owner_rows = (asked_flat[None, :] == jnp.arange(owned_count, dtype=jnp.int32)[:, None]).astype(
-        jnp.bfloat16
-    )
-    grad_states = jnp.dot(
-        owner_rows,
-        returned.reshape(slot_count, local_len * enc_width),
-        preferred_element_type=jnp.float32,
-    )
-    grad_states = grad_states.astype(jnp.bfloat16).reshape(nb_states.shape)
-    return (attn_out, grad_queries, grad_states, grad_w[0], grad_w[1])
+    grad_key_w = grad_key_w.astype(F32).reshape(key_weight.shape)
+    grad_value_w = grad_value_w.astype(F32).reshape(value_weight.shape)
+    return (attn_out, grad_queries, grad_states, grad_key_w, grad_value_w)
 
 
 def solution(mesh):

time: 198 us -> 177 us (0.89)
  Pallas kernels: 111 us -> 163 us
  waiting for transfers between devices: 37.2 us -> 0 us
  blocking collectives: 15.4 us -> 0 us
  starting transfers between devices: 12.8 us -> 0 us
  local copies, waits for them, and re-layouts: 16.2 us -> 6.17 us
  other arithmetic: 0.98 us -> 4.79 us
    pallas_call x1, Pallas kernels: 111 us -> 163 us  [layer(): pl.pallas_call(kernel, out_shape=(jax.ShapeDtypeStruct((rows, cols), BF16...]
    all_to_all x2 -> x0, waiting for transfers between devices: 37.2 us -> none  [the longest x1 20.6 us: body(): lax.all_to_all(outgoing, 'dp', split_axis=0, concat_axis=0, tiled=True)]
    all_to_all x1 -> x0, blocking collectives: 15.4 us -> none  [body(): lax.all_to_all(request, 'dp', split_axis=0, concat_axis=0, tiled=True)]
    all_to_all x2 -> x0, starting transfers between devices: 12.8 us -> none  [the longest x1 7.64 us: body(): lax.all_to_all(outgoing_grad, 'dp', split_axis=0, concat_axis=0, tiled=True)]
    unnamed x19 -> x15, local copies, waits for them, and re-layouts: 8 us -> 4.02 us
    reshape x0 -> x2, other arithmetic: none -> 3.97 us  [the longest x1 2.56 us: body(): grad_key_w = grad_key_w.astype(F32).reshape(key_weight.shape)]
    slice x1 -> x0, local copies, waits for them, and re-layouts: 3.96 us -> none  [body(): return (attn_out, grad_queries, grad_states, grad_w[0], grad_w[1])]
  transfers between devices with their start and end apart: 2 -> 0, of which waited for: 2 -> 0; matrix products, arithmetic and copies ran while one was open for 2% -> 0% of each run, Pallas kernels for 0% -> 0%
where the time goes in v2:
time: 177 us; the launch traced here: 175 us
  Pallas kernels  163 us (92%)
  local copies, waits for them, and re-layouts  6.17 us (3%)
  other arithmetic  4.79 us (3%)
    pallas_call x1, Pallas kernels, layer(): pl.pallas_call(kernel, out_shape=(jax.ShapeDtypeStruct((rows, cols), BF16...  163 us
    unnamed x15, local copies, waits for them, and re-layouts  4.02 us

profile of v2, /device:TPU:32, one launch (start us, length us, event | category | flops | bytes accessed | tf_op | source)
XLA Modules:
  0.0 174.9 jit_solution(16463853189932155272)
XLA Ops:
  0.6 1.3 reshape.65.refs_6_
  1.9 0.8 copy.19
  2.7 0.1 reshape.63
  2.8 0.2 select_reduce_fusion.2
  3.0 0.0 copy-start.4
  3.0 0.8 copy.20
  3.7 0.1 broadcast_in_dim.39
  3.8 0.1 select_reduce_fusion
  3.9 0.5 broadcast_subtract_fusion.refs_1_
  4.4 0.1 reshape.64
  4.5 0.6 pad.4.refs_2_
  5.2 0.0 copy-done.4
  5.2 163.3 %shard_map.119 = (bf16[704,512]{1,0:T(8,128)(2,1)}, bf16[704,512]{1,0:T(8,128)(2,1)}, bf16[16,16,768]{2,1,0:T(8,128)(2,1)}, bf16[8,2,48,512]{3,2,1,0:T(8,128)(2,1)}, bf16[8,2,48,512]{3,2,1,0:T(8,128)(2,1)}) custom-call(s32[22]{0:T(128)} %copy-done.4, s32[64]{0:T(128)} %broadcast_subtract_fusion.refs_1_, s32[32,1,128]{2,1,0:T(1,128)} %pad.4.refs_2_, ...), custom_call_target="tpu_custom_call" | custom-call | flops 14000000000 | bytes 20000000 | tf_op jit(solution)/shard_map/pallas_call | solution.py:448
  168.5 0.0 copy-start
  168.5 2.6 %bitcast_convert_fusion.1 = f32[768,512]{1,0:T(8,128)} fusion(bf16[8,2,48,512]{3,2,1,0:T(8,128)(2,1)} %get-tuple-element.13), kind=kLoop, calls=%fused_computation.1 | loop fusion | flops 393216 | bytes 2359296 | tf_op jit(solution)/shard_map/reshape | solution.py:547
  171.0 0.0 copy-done
  171.0 0.0 copy-start.2
  171.0 0.0 copy-start.1
  171.0 1.4 bitcast_convert_fusion
  172.5 0.0 copy-done.2
  172.5 0.0 copy-start.3
  172.5 0.9 copy.25
  173.3 0.0 copy-done.1
  173.3 0.9 copy.26
  174.2 0.0 copy-done.3
  174.2 0.7 copy.27
  (2 shorter events, 0.0 us)
Async XLA Ops:
  3.0 2.2 %copy-start.4 = (s32[22]{0:T(128)}, s32[22]{0:T(128)S(1)}, u32[]{:S(2)}) copy-start(s32[22]{0:T(128)S(1)} %get-tuple-element.16.refs_0_) | copy-start | bytes 268
  168.5 2.6 %copy-start = (bf16[8,2,48,512]{3,2,1,0:T(8,128)(2,1)S(1)}, bf16[8,2,48,512]{3,2,1,0:T(8,128)(2,1)}, u32[]{:S(2)}) copy-start(bf16[8,2,48,512]{3,2,1,0:T(8,128)(2,1)} %get-tuple-element.14) | copy-start | bytes 2359300
  171.0 1.4 copy-start.2
  171.0 2.3 %copy-start.1 = (bf16[704,512]{1,0:T(8,128)(2,1)S(1)}, bf16[704,512]{1,0:T(8,128)(2,1)}, u32[]{:S(2)}) copy-start(bf16[704,512]{1,0:T(8,128)(2,1)} %get-tuple-element.25) | copy-start | bytes 2162692
  172.5 1.7 copy-start.3

commit v3 on v2

--- a/solution.py
+++ b/solution.py
@@ -47,15 +47,24 @@
     slot_of,
     source_of,
     request,
+    gain,
+    states_hbm,
+    queries_hbm,
+    grads_hbm,
+    key_w_hbm,
+    value_w_hbm,
+    grad_states,
+    attn_hbm,
+    grad_q_hbm,
+    grad_key_w_hbm,
+    grad_value_w_hbm,
     states,
     queries,
     grads,
-    gain,
     key_w,
     value_w,
     attn_out,
     grad_q,
-    grad_states,
     grad_key_w,
     grad_value_w,
     asked,
@@ -63,6 +72,7 @@
     stage,
     fetched,
     mine,
+    back,
     grad_raw,
     returned,
     slot_rows,
@@ -77,11 +87,15 @@
     far_a,
     far_b,
     w_terms,
-    w_slots,
-    w_half,
+    w_big,
+    w_mid,
+    w_small,
+    w_piece,
     w_other,
-    w_mine,
-    w_back,
+    w_done,
+    w_near,
+    w_quarter,
+    w_far,
     left_sem,
     right_sem,
     half_sem,
@@ -91,7 +105,10 @@
     second_sem,
     w_sem,
     out_sem,
+    swap_out,
+    w_out,
     near_sem,
+    local_sem,
 ):
     me_dp = lax.axis_index("dp")
     me_t = lax.axis_index("tensor")
@@ -104,8 +121,40 @@
     mate = {"dp": place * 2 + 1 - low}
     groups = 2 * places
 
-    def place_at(k):
-        return lax.rem(place + k, places)
+    y, x = place // 4, lax.rem(place, 4)
+
+    first_at, second_at = (x, y), (y, x)
+
+    def along(axis, d):
+        if axis == 0:
+            return {"dp": (y * 4 + lax.rem(x + d, 4)) * 2 + low}
+        return {"dp": (lax.rem(y + d, 4) * 4 + x) * 2 + low}
+
+    loads = [
+        pltpu.make_async_copy(src, dst, local_sem.at[n])
+        for n, (src, dst) in enumerate(
+            (
+                (states_hbm, states),
+                (queries_hbm, queries),
+                (grads_hbm, grads),
+                (key_w_hbm, key_w),
+                (value_w_hbm, value_w),
+            )
+        )
+    ]
+    stores = [
+        pltpu.make_async_copy(src, dst, local_sem.at[5 + n])
+        for n, (src, dst) in enumerate(
+            (
+                (attn_out, attn_hbm),
+                (grad_q, grad_q_hbm),
+                (grad_key_w, grad_key_w_hbm),
+                (grad_value_w, grad_value_w_hbm),
+            )
+        )
+    ]
+    for load in loads:
+        load.start()
 
     def ahead(k):
         return {"dp": lax.rem(me_dp + k, groups)}
@@ -137,6 +186,10 @@
     to_scalars.start()
     to_scalars.wait()
 
+    width = states.shape[2]
+    others = pl.ds(0, 2 * (groups - 1))
+    loads[0].wait()
+
     def answer(k, carry):
         for r in range(2):
             stage[2 * (k - 1) + r] = states[asked_s[k - 1, 0, r]]
@@ -147,12 +200,13 @@
     lax.fori_loop(1, groups, answer, 0)
     for r in range(2):
         fetched[2 * (groups - 1) + r] = states[asked_s[groups - 1, 0, r]]
-    others = pl.ds(0, 2 * (groups - 1))
+    for load in loads[1:]:
+        load.wait()
     drain(fetched.at[others], near_sem.at[4])
 
-    gain_row = gain[...]
+    gain_row = gain[...].reshape(1, width)
     span_len = queries.shape[0] // spans
-    local_len, width = mine.shape[1], mine.shape[2]
+    local_len = states.shape[1]
     tokens = per * 2 * RINGS * local_len
     cols = queries.shape[1]
 
@@ -182,10 +236,10 @@
             drain(from_left, left_sem.at[j])
             one = full.at[j * per, l_ring, core]
             send(one, one, out_sem.at[3], half_sem.at[j], right)
-            send(from_left, from_left, out_sem.at[5], core_sem.at[j], twin)
             drain(from_right, right_sem.at[j])
             two = full.at[j * per + 1, r_ring, core]
             send(two, two, out_sem.at[4], half_sem.at[j], left)
+            send(from_left, from_left, out_sem.at[5], core_sem.at[j], twin)
             send(from_right, from_right, out_sem.at[6], core_sem.at[j], twin)
 
         k = i - 4
@@ -202,7 +256,8 @@
         def _():
             at = rows_of(c)
             drain(full.at[at, :, 1 - core], core_sem.at[c])
-            unit, _ = normalize(full[at].reshape(tokens, width))
+            raw = full[at].reshape(tokens, width)
+            unit, _ = normalize(raw)
             encoded = (unit * gain_row).astype(BF16)
             enc_t[:, pl.ds(pl.multiple_of(c * tokens, tokens), tokens)] = encoded.T
             keys = dot(encoded, key_w[...], 1, 0).astype(BF16)
@@ -227,6 +282,8 @@
         return carry
 
     lax.fori_loop(0, spans + 5, gather_step, 0)
+    stores[0].start()
+    stores[1].start()
 
     tile = 256
     tiles = width // tile
@@ -239,22 +296,11 @@
         row = pl.multiple_of(n * tile, tile)
         w_terms[pl.ds(row, tile), :] = dot(left_side, grad_kv[:, lanes], 1, 0).astype(BF16)
 
-    piece = w_slots.shape[1]
-    half = piece // 2
-
-    def piece_rows(p):
-        return pl.ds(pl.multiple_of(p * piece, piece), piece)
-
-    def scatter(k, carry):
-        p = place_at(k)
-        send(
-            w_terms.at[piece_rows(p)],
-            w_slots.at[k - 1],
-            out_sem.at[8],
-            w_sem.at[0],
-            {"dp": p * 2 + low},
-        )
-        return carry
+    quarter = width // 4
+    piece = quarter // 4
+
+    def quarter_rows(part, a):
+        return pl.ds(pl.multiple_of(part * width + a * quarter, quarter), quarter)
 
     def reduce_step(i, carry):
         @pl.when(i < spans)
@@ -267,7 +313,7 @@
             send(
                 term.at[at, :, 1 - core],
                 from_core.at[at],
-                out_sem.at[9],
+                swap_out.at[0],
                 swap_sem.at[i],
                 twin,
             )
@@ -280,9 +326,9 @@
             drain(from_core.at[at], swap_sem.at[j])
             total = term[at, :, core].astype(F32) + from_core[at].astype(F32)
             sums[at] = total.astype(BF16)
-            send(sums.at[j * per, o_ring], near_a.at[j], out_sem.at[10], first_sem.at[0, j], right)
+            send(sums.at[j * per, o_ring], near_a.at[j], swap_out.at[1], first_sem.at[0, j], right)
             send(
-                sums.at[j * per + 1, o_ring], near_b.at[j], out_sem.at[11], first_sem.at[1, j], left
+                sums.at[j * per + 1, o_ring], near_b.at[j], swap_out.at[2], first_sem.at[1, j], left
             )
 
         k = i - 3
@@ -293,50 +339,89 @@
             drain(near_a.at[k], first_sem.at[0, k])
             total = sums[k * per, r_ring].astype(F32) + near_a[k].astype(F32)
             sums[k * per, r_ring] = total.astype(BF16)
-            send(sums.at[at, r_ring], far_a.at[at], out_sem.at[12], second_sem.at[0, k], right)
+            send(sums.at[at, r_ring], far_a.at[at], swap_out.at[3], second_sem.at[0, k], right)
             drain(near_b.at[k], first_sem.at[1, k])
             total = sums[k * per + 1, l_ring].astype(F32) + near_b[k].astype(F32)
             sums[k * per + 1, l_ring] = total.astype(BF16)
-            send(sums.at[at, l_ring], far_b.at[at], out_sem.at[13], second_sem.at[1, k], left)
-
-        @pl.when(i < 3)
+            send(sums.at[at, l_ring], far_b.at[at], swap_out.at[4], second_sem.at[1, k], left)
+
+        @pl.when((i == 2) | (i == 3))
         def _():
             def tile_step(n, carry):
-                weight_tile(2 * i + n)
+                weight_tile(tiles * (i - 2) + n)
                 return carry
 
-            lax.fori_loop(0, 2, tile_step, 0)
-
-        @pl.when(i == 2)
-        def _():
-            lax.fori_loop(1, places, scatter, 0)
+            lax.fori_loop(0, tiles, tile_step, 0)
+
+        @pl.when(i == 3)
+        def _():
+            for d in (1, 2, 3):
+                for part in range(2):
+                    send(
+                        w_terms.at[quarter_rows(part, lax.rem(first_at[part] + d, 4))],
+                        w_big.at[part, d - 1],
+                        w_out.at[0],
+                        w_sem.at[0],
+                        along(part, d),
+                    )
+
+        @pl.when(i == 7)
+        def _():
+            drain(w_big, w_sem.at[0])
+            for part in range(2):
+                total = w_terms[quarter_rows(part, first_at[part]), :].astype(F32)
+                for d in range(3):
+                    total = total + w_big[part, d].astype(F32)
+                w_mid[part] = total.astype(BF16).reshape(4, piece, cols)
+                for d in (1, 2, 3):
+                    send(
+                        w_mid.at[part, lax.rem(second_at[part] + d, 4)],
+                        w_small.at[part, d - 1],
+                        w_out.at[1],
+                        w_sem.at[1],
+                        along(1 - part, d),
+                    )
 
         @pl.when(i == 8)
         def _():
-            drain(w_slots, w_sem.at[0])
-            total = w_terms[piece_rows(place), :].astype(F32)
-            for s in range(places - 1):
-                total = total + w_slots[s].astype(F32)
-            w_half[...] = total.astype(BF16).reshape(2, half, cols)
-            send(w_half.at[1 - low], w_other, out_sem.at[14], w_sem.at[1], mate)
+            drain(w_small, w_sem.at[1])
+            for part in range(2):
+                total = w_mid[part, second_at[part]].astype(F32)
+                for d in range(3):
+                    total = total + w_small[part, d].astype(F32)
+                w_piece[part] = total.astype(BF16)
+            send(w_piece, w_other, w_out.at[2], w_sem.at[2], mate)
 
         @pl.when(i == 9)
         def _():
-            drain(w_other, w_sem.at[1])
-            total = w_half[low].astype(F32) + w_other[...].astype(F32)
-            w_mine[low] = total.astype(BF16)
-            send(w_mine.at[low], w_mine.at[low], out_sem.at[15], w_sem.at[2], mate)
+            drain(w_other, w_sem.at[2])
+            for part in range(2):
+                total = w_piece[part].astype(F32) + w_other[part].astype(F32)
+                w_done[part] = total.astype(BF16)
+                w_quarter[part, second_at[part]] = total.astype(BF16)
+                for d in (1, 2, 3):
+                    send(
+                        w_done.at[part],
+                        w_near.at[part, d - 1],
+                        w_out.at[3],
+                        w_sem.at[3],
+                        along(1 - part, d),
+                    )
 
         @pl.when(i == 10)
         def _():
-            drain(w_mine.at[1 - low], w_sem.at[2])
-
-            def spread(k, carry):
-                device = {"dp": place_at(k) * 2 + low}
-                send(w_mine, w_back.at[k - 1], out_sem.at[16], w_sem.at[3], device)
-                return carry
-
-            lax.fori_loop(1, places, spread, 0)
+            drain(w_near, w_sem.at[3])
+            for part in range(2):
+                for d in (1, 2, 3):
+                    w_quarter[part, lax.rem(second_at[part] + 4 - d, 4)] = w_near[part, d - 1]
+                for d in (1, 2, 3):
+                    send(
+                        w_quarter.at[part],
+                        w_far.at[part, d - 1],
+                        w_out.at[4],
+                        w_sem.at[4],
+                        along(part, d),
+                    )
 
         c = i - 5
 
@@ -358,13 +443,12 @@
 
     asked_count = spans * per
     grad_raw[asked_count] = jnp.zeros((local_len, width), BF16)
-    drain(stage.at[others], near_sem.at[3])
 
     def give_back(k, carry):
         for r in range(2):
-            stage[2 * (k - 1) + r] = grad_raw[source_of[2 * (k - 1) + r]]
+            back[2 * (k - 1) + r] = grad_raw[source_of[2 * (k - 1) + r]]
         at = pl.ds(2 * (k - 1), 2)
-        send(stage.at[at], returned.at[at], near_sem.at[5], near_sem.at[6], ahead(k))
+        send(back.at[at], returned.at[at], near_sem.at[5], near_sem.at[6], ahead(k))
         return carry
 
     lax.fori_loop(1, groups, give_back, 0)
@@ -379,24 +463,13 @@
 
     lax.fori_loop(0, groups, name_rows, 0)
 
-    drain(w_back, w_sem.at[3])
-
-    def keep(source, value):
-        @pl.when(source < places // 2)
-        def _():
-            grad_key_w[source] = value
-
-        @pl.when(source >= places // 2)
-        def _():
-            grad_value_w[source - places // 2] = value
-
-    keep(place, w_mine[...])
-
-    def settle(k, carry):
-        keep(lax.rem(place + places - k, places), w_back[k - 1])
-        return carry
-
-    lax.fori_loop(1, places, settle, 0)
+    drain(w_far, w_sem.at[4])
+    for part, out in enumerate((grad_key_w, grad_value_w)):
+        out[first_at[part]] = w_quarter[part].reshape(quarter, cols).astype(F32)
+        for d in (1, 2, 3):
+            value = w_far[part, d - 1].reshape(quarter, cols).astype(F32)
+            out[lax.rem(first_at[part] + 4 - d, 4)] = value
+        stores[2 + part].start()
 
     slot_tokens = 2 * groups * local_len
     owned = states.shape[0] * local_len
@@ -410,20 +483,22 @@
     grad_states[...] = total.astype(BF16).reshape(states.shape)
 
     drain(remote_asked, near_sem.at[0])
-    drain(stage.at[others], near_sem.at[5])
+    drain(stage.at[others], near_sem.at[3])
+    drain(back.at[others], near_sem.at[5])
+    few = mine.at[pl.ds(0, spans)]
     for n in (0, 1, 2, 5, 6, 7):
         drain(mine, out_sem.at[n])
-    drain(near_a, out_sem.at[3])
-    drain(near_a, out_sem.at[4])
-    drain(w_slots, out_sem.at[8])
-    drain(from_core, out_sem.at[9])
-    drain(near_a, out_sem.at[10])
-    drain(near_b, out_sem.at[11])
-    drain(far_a, out_sem.at[12])
-    drain(far_b, out_sem.at[13])
-    drain(w_other, out_sem.at[14])
-    drain(w_other, out_sem.at[15])
-    drain(w_back, out_sem.at[16])
+    drain(few, out_sem.at[3])
+    drain(few, out_sem.at[4])
+    drain(from_core, swap_out.at[0])
+    drain(near_a, swap_out.at[1])
+    drain(near_b, swap_out.at[2])
+    drain(far_a, swap_out.at[3])
+    drain(far_b, swap_out.at[4])
+    for n, ref in enumerate((w_big, w_small, w_other, w_near, w_far)):
+        drain(ref, w_out.at[n])
+    for store in stores:
+        store.wait()
 
 
 def layer(
@@ -437,31 +512,42 @@
     rows, cols = queries.shape
     places = groups // 2
     tokens = asked * local_len * RINGS * 2
-    piece = 2 * width // places
+    quarter, piece = width // 4, width // 16
 
     def kernel(*refs):
         layer_kernel(spans, per, places, *refs)
 
     vmem = pl.BlockSpec(memory_space=pltpu.VMEM)
     smem = pl.BlockSpec(memory_space=pltpu.SMEM)
+    anywhere = pl.BlockSpec(memory_space=pl.ANY)
     dma = pltpu.SemaphoreType.DMA
     return pl.pallas_call(
         kernel,
         out_shape=(
+            jax.ShapeDtypeStruct((owned, local_len, width), BF16),
             jax.ShapeDtypeStruct((rows, cols), BF16),
             jax.ShapeDtypeStruct((rows, cols), BF16),
-            jax.ShapeDtypeStruct((owned, local_len, width), BF16),
-            jax.ShapeDtypeStruct((places // 2, 2, piece // 2, cols), BF16),
-            jax.ShapeDtypeStruct((places // 2, 2, piece // 2, cols), BF16),
+            jax.ShapeDtypeStruct((4, quarter, cols), F32),
+            jax.ShapeDtypeStruct((4, quarter, cols), F32),
         ),
-        in_specs=[smem] * 2 + [vmem] * 7,
-        out_specs=(vmem,) * 5,
+        in_specs=[smem] * 2 + [vmem] * 2 + [anywhere] * 5,
+        out_specs=(vmem,) + (anywhere,) * 4,
         scratch_shapes=[
+            pltpu.VMEM((owned, local_len, width), BF16),
+            pltpu.VMEM((rows, cols), BF16),
+            pltpu.VMEM((rows, cols), BF16),
+            pltpu.VMEM((width, cols), BF16),
+            pltpu.VMEM((width, cols), BF16),
+            pltpu.VMEM((rows, cols), BF16),
+            pltpu.VMEM((rows, cols), BF16),
+            pltpu.VMEM((4, quarter, cols), F32),
+            pltpu.VMEM((4, quarter, cols), F32),
             pltpu.VMEM((groups, 1, 128), jnp.int32),
             pltpu.SMEM((groups, 1, 128), jnp.int32),
             pltpu.VMEM((2 * groups, local_len, width), BF16),
             pltpu.VMEM((2 * groups, local_len, width), BF16),
             pltpu.VMEM((asked, local_len, width), BF16),
+            pltpu.VMEM((2 * groups, local_len, width), BF16),
             pltpu.VMEM((asked + 1, local_len, width), BF16),
             pltpu.VMEM((2 * groups, local_len, width), BF16),
             pltpu.VMEM((2 * groups * local_len, owned * local_len), jnp.int32),
@@ -476,11 +562,15 @@
             pltpu.VMEM((asked, local_len, width), BF16),
             pltpu.VMEM((asked, local_len, width), BF16),
             pltpu.VMEM((2 * width, cols), BF16),
-            pltpu.VMEM((places - 1, piece, cols), BF16),
-            pltpu.VMEM((2, piece // 2, cols), BF16),
-            pltpu.VMEM((piece // 2, cols), BF16),
-            pltpu.VMEM((2, piece // 2, cols), BF16),
-            pltpu.VMEM((places - 1, 2, piece // 2, cols), BF16),
+            pltpu.VMEM((2, 3, quarter, cols), BF16),
+            pltpu.VMEM((2, 4, piece, cols), BF16),
+            pltpu.VMEM((2, 3, piece, cols), BF16),
+            pltpu.VMEM((2, piece, cols), BF16),
+            pltpu.VMEM((2, piece, cols), BF16),
+            pltpu.VMEM((2, piece, cols), BF16),
+            pltpu.VMEM((2, 3, piece, cols), BF16),
+            pltpu.VMEM((2, 4, piece, cols), BF16),
+            pltpu.VMEM((2, 3, 4, piece, cols), BF16),
             dma((spans,)),
             dma((spans,)),
             dma((spans,)),
@@ -488,9 +578,12 @@
             dma((spans,)),
             dma((2, spans)),
             dma((2, spans)),
-            dma((4,)),
-            dma((17,)),
+            dma((5,)),
+            dma((8,)),
+            dma((5,)),
+            dma((5,)),
             dma((7,)),
+            dma((9,)),
         ],
         compiler_params=pltpu.CompilerParams(
             collective_id=0, has_side_effects=True, vmem_limit_bytes=58 * 1024 * 1024
@@ -502,10 +595,10 @@
         slot_of,
         source_of,
         request,
+        enc_gain,
         states,
         queries,
         grad_attn,
-        enc_gain.reshape(1, width),
         key_weight,
         value_weight,
     )
@@ -529,11 +622,11 @@
     source_of = asked_count - jnp.sum(
         jnp.where(filled, asked_count - positions[:, None], 0), axis=0
     ).astype(jnp.int32)
-    owner_rank = owner_list * capacity + slot_rank
-    named = owner_rank[:, None] == slots[None, :]
-    request = jnp.sum(jnp.where(named, row_list[:, None], 0), axis=0).astype(jnp.int32)
-    request = jnp.pad(request.reshape(groups, 1, capacity), ((0, 0), (0, 0), (0, 128 - capacity)))
-    attn_out, grad_queries, grad_states, grad_key_w, grad_value_w = layer(
+    asked_of = owner_list[:, None, None] == jnp.arange(groups, dtype=jnp.int32)[None, :, None]
+    rank_is = slot_rank[:, None, None] == jnp.arange(128, dtype=jnp.int32)[None, None, :]
+    request = jnp.sum(jnp.where(asked_of & rank_is, row_list[:, None, None], 0), axis=0)
+    request = request.astype(jnp.int32).reshape(groups, 1, 128)
+    grad_states, attn_out, grad_queries, grad_key_w, grad_value_w = layer(
         slot_of,
         source_of,
         request,
@@ -544,8 +637,8 @@
         key_weight,
         value_weight,
     )
-    grad_key_w = grad_key_w.astype(F32).reshape(key_weight.shape)
-    grad_value_w = grad_value_w.astype(F32).reshape(value_weight.shape)
+    grad_key_w = grad_key_w.reshape(key_weight.shape)
+    grad_value_w = grad_value_w.reshape(value_weight.shape)
     return (attn_out, grad_queries, grad_states, grad_key_w, grad_value_w)
 
 

time: 177 us -> 166 us (0.938)
  Pallas kernels: 163 us -> 153 us
  other arithmetic: 4.79 us -> 1.75 us
  local copies, waits for them, and re-layouts: 6.17 us -> 8.61 us
    pallas_call x1, Pallas kernels: 163 us -> 153 us  [layer(): pl.pallas_call(kernel, out_shape=(jax.ShapeDtypeStruct((owned, local_len,...]
    unnamed x15 -> x17, local copies, waits for them, and re-layouts: 4.02 us -> 8.44 us
    reshape x2 -> x0, other arithmetic: 3.97 us -> none  [the longest x1 2.56 us: body(): grad_key_w = grad_key_w.astype(F32).reshape(key_weight.shape)]
where the time goes in v3:
time: 166 us; the launch traced here: 164 us
  Pallas kernels  153 us (92%)
  local copies, waits for them, and re-layouts  8.61 us (5%)
  other arithmetic  1.75 us (1%)
    pallas_call x1, Pallas kernels, layer(): pl.pallas_call(kernel, out_shape=(jax.ShapeDtypeStruct((owned, local_len,...  153 us
    unnamed x17, local copies, waits for them, and re-layouts  8.44 us

profile of v3, /device:TPU:32, one launch (start us, length us, event | category | flops | bytes accessed | tf_op | source)
XLA Modules:
  0.0 164.5 jit_solution(6442404571685327393)
XLA Ops:
  0.6 0.8 copy.17
  1.4 0.1 reshape.95
  1.5 0.2 select_reduce_fusion.2
  1.7 0.0 copy-start.4
  1.7 0.1 select_reduce_fusion.1
  1.8 0.5 broadcast_subtract_fusion.refs_1_
  2.3 0.1 iota_compare_fusion.1
  2.4 0.1 iota_compare_fusion
  2.5 0.8 copy.18
  3.2 0.1 broadcast_in_dim.46
  3.3 0.8 select_reduce_fusion
  4.1 0.0 copy-done.4
  4.1 153.4 %shard_map.119 = (bf16[16,16,768]{2,1,0:T(8,128)(2,1)}, bf16[704,512]{1,0:T(8,128)(2,1)}, bf16[704,512]{1,0:T(8,128)(2,1)}, f32[4,192,512]{2,1,0:T(8,128)}, f32[4,192,512]{2,1,0:T(8,128)}) custom-call(s32[22]{0:T(128)} %copy-done.4, s32[64]{0:T(128)} %broadcast_subtract_fusion.refs_1_, s32[32,1,128]{2,1,0:T(1,128)} %bitcast.5, f32[768]{0:T(1024)} %refs_3_.1, ...), custom_call_target="tpu_custom_call" | custom-call | flops 14000000000 | bytes 20000000 | tf_op jit(solution)/shard_map/pallas_call | solution.py:524
  157.5 0.0 copy-start.2
  157.5 0.0 copy-start.3
  157.5 0.0 copy-start.1
  157.6 2.2 %copy.24 = bf16[704,512]{1,0:T(8,128)(2,1)} copy(bf16[704,512]{1,0:T(8,128)(2,1)} %get-tuple-element.22) | data formatting | bytes 1441792
  159.7 0.0 copy-done.2
  159.7 0.9 copy.25
  160.6 0.0 copy-done.3
  160.6 0.7 copy.26
  161.3 0.0 copy-done.1
  161.3 0.0 copy-start
  161.3 1.1 copy.27
  162.5 0.8 copy-done
  163.3 1.1 copy.28
  (1 shorter events, 0.0 us)
Async XLA Ops:
  1.7 2.4 %copy-start.4 = (s32[22]{0:T(128)}, s32[22]{0:T(128)S(1)}, u32[]{:S(2)}) copy-start(s32[22]{0:T(128)S(1)} %get-tuple-element.15.refs_0_) | copy-start | bytes 268
  157.5 2.2 %copy-start.2 = (bf16[704,512]{1,0:T(8,128)(2,1)S(1)}, bf16[704,512]{1,0:T(8,128)(2,1)}, u32[]{:S(2)}) copy-start(bf16[704,512]{1,0:T(8,128)(2,1)} %get-tuple-element.23) | copy-start | bytes 2162692
  157.5 3.0 %copy-start.3 = (bf16[16,16,768]{2,1,0:T(8,128)(2,1)S(1)}, bf16[16,16,768]{2,1,0:T(8,128)(2,1)}, u32[]{:S(2)}) copy-start(bf16[16,16,768]{2,1,0:T(8,128)(2,1)} %get-tuple-element.24) | copy-start | bytes 1179652
  157.5 3.8 %copy-start.1 = (f32[4,192,512]{2,1,0:T(8,128)S(1)}, f32[4,192,512]{2,1,0:T(8,128)}, u32[]{:S(2)}) copy-start(f32[4,192,512]{2,1,0:T(8,128)} %get-tuple-element.13) | copy-start | bytes 4718596
  161.3 2.0 %copy-start = (f32[4,192,512]{2,1,0:T(8,128)S(1)}, f32[4,192,512]{2,1,0:T(8,128)}, u32[]{:S(2)}) copy-start(f32[4,192,512]{2,1,0:T(8,128)} %get-tuple-element.14) | copy-start | bytes 4718596

commit v4 on v3

--- a/solution.py
+++ b/solution.py
@@ -213,6 +213,22 @@
     def rows_of(c):
         return pl.ds(c * per, per)
 
+    early = spans // 2 + 1
+
+    def encoder_term(c):
+        t_rows = pl.ds(pl.multiple_of(c * tokens, tokens), tokens)
+        product = dot(grad_kv[t_rows, :cols], key_w[...], 1, 1)
+        product = product + dot(grad_kv[t_rows, cols:], value_w[...], 1, 1)
+        at = rows_of(c)
+        term[at] = product.astype(BF16).reshape(per, RINGS, 2, local_len, width)
+        send(
+            term.at[at, :, 1 - core],
+            from_core.at[at],
+            swap_out.at[0],
+            swap_sem.at[c],
+            twin,
+        )
+
     def gather_step(i, carry):
         @pl.when(i < spans)
         def _():
@@ -279,6 +295,10 @@
                 v_lanes = slice(cols + h * HEAD_DIM, cols + (h + 1) * HEAD_DIM)
                 grad_kv[t_rows, v_lanes] = dot(w, g, 0, 0).astype(BF16)
 
+        @pl.when((c >= 0) & (c < early))
+        def _():
+            encoder_term(c)
+
         return carry
 
     lax.fori_loop(0, spans + 5, gather_step, 0)
@@ -303,20 +323,9 @@
         return pl.ds(pl.multiple_of(part * width + a * quarter, quarter), quarter)
 
     def reduce_step(i, carry):
-        @pl.when(i < spans)
-        def _():
-            t_rows = pl.ds(pl.multiple_of(i * tokens, tokens), tokens)
-            product = dot(grad_kv[t_rows, :cols], key_w[...], 1, 1)
-            product = product + dot(grad_kv[t_rows, cols:], value_w[...], 1, 1)
-            at = rows_of(i)
-            term[at] = product.astype(BF16).reshape(per, RINGS, 2, local_len, width)
-            send(
-                term.at[at, :, 1 - core],
-                from_core.at[at],
-                swap_out.at[0],
-                swap_sem.at[i],
-                twin,
-            )
+        @pl.when((i >= early) & (i < spans))
+        def _():
+            encoder_term(i)
 
         j = i - 1
 

time: 166 us -> 161 us (0.970)
  Pallas kernels: 153 us -> 150 us
    pallas_call x1, Pallas kernels: 153 us -> 150 us  [layer(): pl.pallas_call(kernel, out_shape=(jax.ShapeDtypeStruct((owned, local_len,...]
where the time goes in v4:
time: 161 us
  Pallas kernels  150 us (93%)
  local copies, waits for them, and re-layouts  8.61 us (5%)
  other arithmetic  1.75 us (1%)
    pallas_call x1, Pallas kernels, layer(): pl.pallas_call(kernel, out_shape=(jax.ShapeDtypeStruct((owned, local_len,...  150 us
    unnamed x17, local copies, waits for them, and re-layouts  8.44 us

profile of v4, /device:TPU:32, one launch (start us, length us, event | category | flops | bytes accessed | tf_op | source)
XLA Modules:
  0.0 160.7 jit_solution(9845572851435189660)
XLA Ops:
  0.6 0.8 copy.17
  1.4 0.1 reshape.95
  1.5 0.2 select_reduce_fusion.2
  1.7 0.0 copy-start.4
  1.7 0.1 select_reduce_fusion.1
  1.8 0.5 broadcast_subtract_fusion.refs_1_
  2.3 0.1 iota_compare_fusion.1
  2.4 0.1 iota_compare_fusion
  2.5 0.8 copy.18
  3.2 0.1 broadcast_in_dim.46
  3.3 0.8 select_reduce_fusion
  4.1 0.0 copy-done.4
  4.1 149.6 %shard_map.119 = (bf16[16,16,768]{2,1,0:T(8,128)(2,1)}, bf16[704,512]{1,0:T(8,128)(2,1)}, bf16[704,512]{1,0:T(8,128)(2,1)}, f32[4,192,512]{2,1,0:T(8,128)}, f32[4,192,512]{2,1,0:T(8,128)}) custom-call(s32[22]{0:T(128)} %copy-done.4, s32[64]{0:T(128)} %broadcast_subtract_fusion.refs_1_, s32[32,1,128]{2,1,0:T(1,128)} %bitcast.5, f32[768]{0:T(1024)} %refs_3_.1, ...), custom_call_target="tpu_custom_call" | custom-call | flops 14000000000 | bytes 20000000 | tf_op jit(solution)/shard_map/pallas_call | solution.py:533
  153.7 0.0 copy-start.2
  153.7 0.0 copy-start.3
  153.8 0.0 copy-start.1
  153.8 2.2 %copy.24 = bf16[704,512]{1,0:T(8,128)(2,1)} copy(bf16[704,512]{1,0:T(8,128)(2,1)} %get-tuple-element.22) | data formatting | bytes 1441792
  155.9 0.0 copy-done.2
  155.9 0.9 copy.25
  156.8 0.0 copy-done.3
  156.8 0.7 copy.26
  157.5 0.0 copy-done.1
  157.5 0.0 copy-start
  157.5 1.1 copy.27
  158.7 0.8 copy-done
  159.5 1.1 copy.28
  (1 shorter events, 0.0 us)
Async XLA Ops:
  1.7 2.4 %copy-start.4 = (s32[22]{0:T(128)}, s32[22]{0:T(128)S(1)}, u32[]{:S(2)}) copy-start(s32[22]{0:T(128)S(1)} %get-tuple-element.15.refs_0_) | copy-start | bytes 268
  153.7 2.2 %copy-start.2 = (bf16[704,512]{1,0:T(8,128)(2,1)S(1)}, bf16[704,512]{1,0:T(8,128)(2,1)}, u32[]{:S(2)}) copy-start(bf16[704,512]{1,0:T(8,128)(2,1)} %get-tuple-element.23) | copy-start | bytes 2162692
  153.7 3.0 %copy-start.3 = (bf16[16,16,768]{2,1,0:T(8,128)(2,1)S(1)}, bf16[16,16,768]{2,1,0:T(8,128)(2,1)}, u32[]{:S(2)}) copy-start(bf16[16,16,768]{2,1,0:T(8,128)(2,1)} %get-tuple-element.24) | copy-start | bytes 1179652
  153.8 3.8 %copy-start.1 = (f32[4,192,512]{2,1,0:T(8,128)S(1)}, f32[4,192,512]{2,1,0:T(8,128)}, u32[]{:S(2)}) copy-start(f32[4,192,512]{2,1,0:T(8,128)} %get-tuple-element.13) | copy-start | bytes 4718596
  157.5 2.0 %copy-start = (f32[4,192,512]{2,1,0:T(8,128)S(1)}, f32[4,192,512]{2,1,0:T(8,128)}, u32[]{:S(2)}) copy-start(f32[4,192,512]{2,1,0:T(8,128)} %get-tuple-element.14) | copy-start | bytes 4718596
